TPU v7x, 32 devices: a whole 2x2x4 slice. The times are simulated.
32 devices in a mesh: replica: 8 (over y, x, core), tensor: 4 (over z).
Axes of the slice: x: 2, y: 2, z: 4, core: 2. Of those that a mesh axis runs over, the one named last changes fastest.
Arguments:
- hidden: bfloat16 [2048, 7168], P('replica', 'tensor'), may hold values from -6 to 6
- out_grad: bfloat16 [2048, 4096], P(('replica', 'tensor')), may hold values from -6 to 6
- weights: bfloat16 [8, 56, 128, 1024], P('replica', 'tensor'), may hold values from -6 to 6
- momentum: bfloat16 [8, 56, 128, 1024], P('replica', 'tensor'), may hold values from -3 to 3
- block_cols: int32 [56, 8], P('tensor'), may hold values from 0 to 31, as said below
- step_number: int32 [1], replicated, may hold values from 0 to 999
Outputs:
- outputs: bfloat16 [2048, 4096], P(('replica', 'tensor'))
- new_weights: bfloat16 [8, 56, 128, 1024], P('replica', 'tensor')
- new_momentum: bfloat16 [8, 56, 128, 1024], P('replica', 'tensor')
Inputs may be any that keep to these rules, and one draw needn't show every extreme that they name: `block_cols`: each row names 8 different column blocks; all replicas share the pattern.
All inputs are finite; a program needn't handle non-finite values.
Results may differ from a plain program's by a relative error of at most 0.013.
Values may be sent and summed in bfloat16 or wider, within the bound.
No kernel may reach another device: no remote copies, remote signals or barrier semaphores. Data moves between devices by JAX's collectives and lax.ppermute only.
A program may use at most 192 MiB of HBM per device.

v0:
```python
import jax
import jax.numpy as jnp
from jax import lax
from jax.sharding import PartitionSpec as P

LAMBDA_DC = 1.0
MOMENT_DECAY = 0.9
LEARN_RATE = 0.2


def for_sending(value):
    return jax.tree.map(lambda a: a.astype(jnp.bfloat16) if a.dtype == jnp.float32 else a, value)


def from_partner(value, axis, distance):
    return lax.ppermute(value, axis, [(i, i ^ 1 << distance) for i in range(lax.axis_size(axis))])


def partner_state(payload, chosen_bit, level_count):

    def branch_for(bit_number):

        def swapped(state):
            return jax.tree.map(
                lambda part, own: part.astype(own.dtype),
                from_partner(for_sending(state), "replica", bit_number),
                state,
            )

        return swapped

    return lax.switch(
        chosen_bit, [branch_for(bit_number) for bit_number in range(level_count)], payload
    )


def apply_update(gradient, own_w, own_m, mate_w, mate_m):
    own_w = own_w.astype(jnp.float32)
    own_m = own_m.astype(jnp.float32)
    mean_w = 0.5 * (own_w + mate_w.astype(jnp.float32))
    mean_m = 0.5 * (own_m + mate_m.astype(jnp.float32))
    corrected = gradient + LAMBDA_DC * gradient * gradient * (mean_w - own_w)
    moment_new = MOMENT_DECAY * mean_m + corrected
    weight_new = mean_w - LEARN_RATE * moment_new
    return (weight_new.astype(jnp.bfloat16), moment_new.astype(jnp.bfloat16))


def body(hidden, out_grad, weights, momentum, block_cols, step_number):
    token_count, unit_count = hidden.shape
    rows_here, model_width = out_grad.shape
    row_blocks = weights.shape[1]
    block_size = weights.shape[2]
    per_row = block_cols.shape[1]
    col_blocks = model_width // block_size
    weight_scale = (4.0 / (unit_count * lax.axis_size("tensor"))) ** 0.5
    local_w = weights[0]
    local_m = momentum[0]
    level_count = lax.axis_size("replica").bit_length() - 1
    chosen_bit = step_number[0] % level_count
    placing = block_cols[:, :, None] == jnp.arange(col_blocks, dtype=jnp.int32)[None, None, :]
    placing_b16 = placing.astype(jnp.bfloat16)
    hid_major = hidden.reshape(token_count, row_blocks, block_size).transpose(1, 0, 2)
    split_w = local_w.reshape(row_blocks, block_size, per_row, block_size)
    dense_w = jnp.einsum(
        "rbkj,rkc->rbcj", split_w, placing_b16, preferred_element_type=jnp.float32
    ).astype(jnp.bfloat16)
    dense_w = dense_w.reshape(unit_count, model_width)
    hid_rows = hidden
    summed = lax.psum_scatter(
        (jnp.dot(hid_rows, dense_w, preferred_element_type=jnp.float32) * weight_scale).astype(
            jnp.bfloat16
        ),
        "tensor",
        scatter_dimension=0,
        tiled=True,
    )
    section = lax.all_gather(out_grad, "tensor", axis=0, tiled=True)
    row_count = section.shape[0]
    hid_rows = hid_major
    section_blocks = section.reshape(row_count, col_blocks, block_size)
    selected = jnp.einsum(
        "tcj,rkc->rtkj", section_blocks, placing_b16, preferred_element_type=jnp.float32
    ).astype(jnp.bfloat16)
    selected = selected.reshape(row_blocks, row_count, per_row * block_size)
    gradient = jnp.einsum("rtb,rtk->rbk", hid_rows, selected, preferred_element_type=jnp.float32)
    outputs, gradient = (summed, gradient * weight_scale)
    mates = partner_state((local_w, local_m), chosen_bit, level_count)
    weight_new, moment_new = apply_update(gradient, local_w, local_m, mates[0], mates[1])
    return (outputs, weight_new[None], moment_new[None])


def solution(mesh):
    return jax.shard_map(
        body,
        mesh=mesh,
        in_specs=(
            P("replica", "tensor"),
            P(("replica", "tensor"), None),
            P("replica", "tensor", None, None),
            P("replica", "tensor", None, None),
            P("tensor", None),
            P(),
        ),
        out_specs=(
            P(("replica", "tensor"), None),
            P("replica", "tensor", None, None),
            P("replica", "tensor", None, None),
        ),
        check_vma=False,
    )
```

profile of v0, /device:TPU:0, one launch (start us, length us, event | category | flops | bytes accessed | tf_op | source)
XLA Modules:
  0.0 129.0 jit_solution(16814342442275756121)
XLA Ops:
  7.2 0.0 all-gather.2.cloned.1.call-start
  7.2 0.7 all-gather.2.cloned.1.call-update
  7.9 0.0 reduce-scatter.4.cloned.1.call-start
  7.9 0.8 copy.42
  8.7 4.8 %copy.71 = bf16[224,8,8,128]{3,2,1,0:T(8,128)(2,1)} copy(bf16[224,8,8,128]{3,1,2,0:T(8,128)(2,1)} %bitcast.74) | data formatting | bytes 7340032
  13.5 0.0 copy-start
  13.5 5.9 %convolution_convert_fusion = bf16[14,32,128,128]{3,1,2,0:T(8,128)(2,1)S(1)} fusion(s32[14,8]{1,0:T(8,128)S(1)} %copy.42, bf16[14,128,8,128]{3,2,1,0:T(8,128)(2,1)} %bitcast.73), kind=kOutput, calls=%fused_computation.3 | convolution fusion | flops 124784128 | bytes 18350528 | tf_op jit(solution)/shard_map/rbkj,rkc->rbcj/dot_general | solution.py:64
  19.5 0.0 copy-done
  19.5 16.6 %fusion.13 = bf16[256,4096]{0,1:T(8,128)(2,1)S(1)} fusion(bf16[256,1792]{1,0:T(8,128)(2,1)S(1)} %copy-done, bf16[224,8,32,128]{3,2,1,0:T(8,128)(2,1)S(1)} %bitcast.71), kind=kOutput, calls=%fused_computation.15 | convolution fusion | flops 3760193536 | bytes 17694720 | tf_op jit(solution)/shard_map/dot_general | solution.py:70
  36.1 3.0 %copy.63 = bf16[256,4096]{1,0:T(8,128)(2,1)} copy(bf16[256,4096]{0,1:T(8,128)(2,1)S(1)} %fusion.13) | data formatting | bytes 4194304
  39.1 0.0 reduce-scatter.4.cloned.1.call-update
  39.8 5.9 %copy.43 = bf16[1,14,128,1024]{2,3,1,0:T(8,128)(2,1)} copy(bf16[1,14,128,1024]{3,2,1,0:T(8,128)(2,1)} %param.11) | data formatting | bytes 7340032 | tf_op args[2]
  45.7 0.5 copy.53
  46.2 5.9 %copy.44 = bf16[1,14,128,1024]{2,3,1,0:T(8,128)(2,1)} copy(bf16[1,14,128,1024]{3,2,1,0:T(8,128)(2,1)} %param.12) | data formatting | bytes 7340032 | tf_op args[3]
  52.2 25.2 %conditional.3 = (f32[14,128,1024]{1,2,0:T(8,128)}, f32[14,128,1024]{1,2,0:T(8,128)}) conditional(s32[]{:T(128)} %clamp.3, (bf16[14,128,1024]{1,2,0:T(8,128)(2,1)}, bf16[14,128,1024]{1,2,0:T(8,128)(2,1)}) %tuple.77, (bf16[14,128,1024]{1,2,0:T(8,128)(2,1)}, bf16[14,128,1024]{1,2,0:T(8,128)(2,1)}) %tuple.78, ...), branch_computations={%region_1.2_spmd, %region_2.3_spmd, %region_3.4_spmd} | conditional | bytes 66060384
  52.2 5.9 %copy.45 = bf16[14,128,1024]{2,1,0:T(8,128)(2,1)} copy(bf16[14,128,1024]{1,2,0:T(8,128)(2,1)} %get-tuple-element.57) | data formatting | bytes 7340032 | tf_op jit(solution)/shard_map
  58.1 0.4 collective-permute-start
  58.5 6.0 %copy.46 = bf16[14,128,1024]{2,1,0:T(8,128)(2,1)} copy(bf16[14,128,1024]{1,2,0:T(8,128)(2,1)} %get-tuple-element.58) | data formatting | bytes 7340032 | tf_op jit(solution)/shard_map
  64.5 0.1 collective-permute-start.1
  64.6 0.4 collective-permute-done
  64.9 6.3 %copy.65 = f32[14,128,1024]{1,2,0:T(8,128)} copy(bf16[14,128,1024]{2,1,0:T(8,128)(2,1)} %collective-permute-done) | data formatting | bytes 11010048 | tf_op jit(solution)/shard_map/conditional.1
  71.2 0.0 collective-permute-done.1
  71.2 6.1 %copy.68 = f32[14,128,1024]{1,2,0:T(8,128)} copy(bf16[14,128,1024]{2,1,0:T(8,128)(2,1)} %collective-permute-done.1) | data formatting | bytes 11010048 | tf_op jit(solution)/shard_map/conditional.1
  77.4 0.0 all-gather.2.cloned.1.call-done
  77.4 2.1 %copy.73 = bf16[32,8,32,128]{3,2,1,0:T(8,128)(2,1)S(1)} copy(bf16[32,8,32,128]{3,1,2,0:T(8,128)(2,1)} %bitcast.77) | data formatting | bytes 4194304
  79.5 5.1 %convert_bitcast_fusion = bf16[14,256,8,128]{3,2,1,0:T(8,128)(2,1)} fusion(bf16[256,32,128,1]{2,1,0,3:T(8,128)(2,1)S(1)} %bitcast.75, s32[14,8]{1,0:T(8,128)S(1)} %copy.42), kind=kOutput, calls=%fused_computation.12 | convolution fusion | flops 238554624 | bytes 9437632 | tf_op jit(solution)/shard_map/tcj,rkc->rtkj/dot_general | solution.py:81
  84.5 11.0 %copy.62 = bf16[14,256,8,128]{1,3,2,0:T(8,128)(2,1)} copy(bf16[14,256,8,128]{3,2,1,0:T(8,128)(2,1)} %convert_bitcast_fusion) | data formatting | bytes 14680064 | tf_op jit(solution)/shard_map/reshape | solution.py:84
  95.6 14.8 %convert_bitcast_fusion.1 = (bf16[1,14,128,1024]{2,3,1,0:T(8,128)(2,1)}, bf16[1,14,128,1024]{2,3,1,0:T(8,128)(2,1)}) fusion(f32[14,128,1024]{1,2,0:T(8,128)} %get-tuple-element.66, bf16[1,14,128,1024]{2,3,1,0:T(8,128)(2,1)} %copy.43, bf16[14,256,1024]{1,2,0:T(8,128)(2,1)} %bitcast.72, bf16[14,256,128]{1,2,0:T(8,128)(2,1)S(1)} %bitcast.76, ...), kind=kOutput, calls=%fused_computation.18 | convolution fusion | flops 968884224 | bytes 37617664 | tf_op jit(solution)/shard_map/rtb,rtk->rbk/dot_general | solution.py:85
  110.3 5.9 %copy.57 = bf16[1,14,128,1024]{3,2,1,0:T(8,128)(2,1)} copy(bf16[1,14,128,1024]{2,3,1,0:T(8,128)(2,1)} %get-tuple-element.69) | data formatting | bytes 7340032
  116.2 5.9 %copy.58 = bf16[1,14,128,1024]{3,2,1,0:T(8,128)(2,1)} copy(bf16[1,14,128,1024]{2,3,1,0:T(8,128)(2,1)} %get-tuple-element.68) | data formatting | bytes 7340032
  122.2 0.0 reduce-scatter.4.cloned.1.call-done
Async XLA Ops:
  7.2 70.2 %all-gather.2.cloned.1.call-start = ((), (), s32[]{:S(2)}) async-start(), calls=%async_computation.1 | async-start | bytes 2621440 | tf_op jit(solution)/shard_map/all_gather | solution.py:77
  7.9 114.3 %reduce-scatter.4.cloned.1.call-start = ((), (), s32[]{:S(2)}) async-start(), calls=%async_computation.2 | async-start | bytes 2621440
  13.5 6.0 %copy-start = (bf16[256,1792]{1,0:T(8,128)(2,1)S(1)}, bf16[256,1792]{1,0:T(8,128)(2,1)}, u32[]{:S(2)}) copy-start(bf16[256,1792]{1,0:T(8,128)(2,1)} %param.9) | copy-start | bytes 2752516
  58.1 6.8 %collective-permute-start = (bf16[14,128,1024]{2,1,0:T(8,128)(2,1)}, bf16[14,128,1024]{2,1,0:T(8,128)(2,1)}, u32[]{:S(2)}, u32[]{:S(2)}) collective-permute-start(bf16[14,128,1024]{2,1,0:T(8,128)(2,1)} %copy.45), channel_id=1, source_target_pairs={{0,4},{4,0},{8,12},{12,8},{16,20},{20,16},{24,28},{28,24},{1,5},{5... | collective-permute-start | bytes 11010056 | tf_op jit(solution)/shard_map/cond/branch_0_fun/ppermute | solution.py:16
  64.5 6.8 %collective-permute-start.1 = (bf16[14,128,1024]{2,1,0:T(8,128)(2,1)}, bf16[14,128,1024]{2,1,0:T(8,128)(2,1)}, u32[]{:S(2)}, u32[]{:S(2)}) collective-permute-start(bf16[14,128,1024]{2,1,0:T(8,128)(2,1)} %copy.46), channel_id=1, source_target_pairs={{0,4},{4,0},{8,12},{12,8},{16,20},{20,16},{24,28},{28,24},{1,5},{5... | collective-permute-start | bytes 11010056 | tf_op jit(solution)/shard_map/cond/branch_0_fun/ppermute | solution.py:16
Sparse Core Ops, SparseCore 0:
  9.6 48.6 all-gather.1
  61.1 42.5 reduce-scatter.3
where the time goes:
time: 131 us; the launch traced here: 129 us
  local copies, waits for them, and re-layouts  70.2 us (54%)
  matrix products  42.4 us (32%)
  between operations  14.7 us (11%)
    unnamed x11, local copies, waits for them, and re-layouts  34.8 us
    another operation x4, local copies, waits for them, and re-layouts  24.3 us
    dot_general x1, matrix products, body(): jnp.dot(hid_rows, dense_w, preferred_element_type=jnp.float32)  16.6 us
    dot_general x1, matrix products, body(): jnp.einsum('rtb,rtk->rbk', hid_rows, selected, preferred_element_type=jnp...  14.8 us
    reshape x1, local copies, waits for them, and re-layouts, body(): selected = selected.reshape(row_blocks, row_count, per_row * block_size)  11 us
    dot_general x1, matrix products, body(): jnp.einsum('rbkj,rkc->rbcj', split_w, placing_b16, preferred_element_type...  5.95 us
    dot_general x1, matrix products, body(): jnp.einsum('tcj,rkc->rtkj', section_blocks, placing_b16, preferred_elemen...  5.06 us
  transfers between devices with their start and end apart: 4, of which 1 were waited for; matrix products, arithmetic and copies ran while one was open for 87% of the time, Pallas kernels for 0%

commit v1 on v0

v1 whole, which is shorter than its diff:
```python
import functools

import jax
import jax.numpy as jnp
from jax import lax
from jax.experimental import pallas as pl
from jax.experimental.pallas import tpu as pltpu
from jax.sharding import PartitionSpec as P

LAMBDA_DC = 1.0
MOMENT_DECAY = 0.9
LEARN_RATE = 0.2
VMEM_LIMIT = 32 * 1024 * 1024


def forward_kernel(scale, shards, me_ref, cols_ref, hid_ref, w_ref, *refs):
    slots, total = refs[:shards], refs[shards]
    step = pl.program_id(0)
    rows_step, block_size = w_ref.shape[0], w_ref.shape[1]
    per_row = w_ref.shape[2] // block_size

    @pl.when(step == 0)
    def _():
        total[...] = jnp.zeros_like(total)

    for i in range(rows_step):
        product = jnp.dot(
            hid_ref[:, i * block_size : (i + 1) * block_size],
            w_ref[i],
            preferred_element_type=jnp.float32,
        )
        for k in range(per_row):
            col = cols_ref[step * rows_step + i, k]
            total[col] += product[:, k * block_size : (k + 1) * block_size]

    @pl.when(step == pl.num_programs(0) - 1)
    def _():
        count = slots[0].shape[0]
        for s in range(shards):
            start = pl.multiple_of(lax.rem(me_ref[0] + s, shards) * count, count)
            for col in range(total.shape[0]):
                piece = total[col, pl.ds(start, count), :] * scale
                slots[s][:, col * block_size : (col + 1) * block_size] = piece.astype(jnp.bfloat16)


def forward_parts(me, cols, hidden, weights, scale, shards, model_width):
    tokens = hidden.shape[0]
    row_blocks, block_size, width = weights.shape
    rows_step = 2 if row_blocks % 2 == 0 else 1
    count = tokens // shards
    return pl.pallas_call(
        functools.partial(forward_kernel, scale, shards),
        out_shape=[jax.ShapeDtypeStruct((count, model_width), jnp.bfloat16)] * shards,
        grid_spec=pltpu.PrefetchScalarGridSpec(
            num_scalar_prefetch=2,
            grid=(row_blocks // rows_step,),
            in_specs=[
                pl.BlockSpec((tokens, rows_step * block_size), lambda r, *_: (0, r)),
                pl.BlockSpec((rows_step, block_size, width), lambda r, *_: (r, 0, 0)),
            ],
            out_specs=[pl.BlockSpec((count, model_width), lambda r, *_: (0, 0))] * shards,
            scratch_shapes=[pltpu.VMEM((model_width // block_size, tokens, block_size), jnp.float32)],
        ),
        compiler_params=pltpu.CompilerParams(vmem_limit_bytes=VMEM_LIMIT),
        cost_estimate=pl.CostEstimate(
            flops=2 * tokens * row_blocks * block_size * width,
            bytes_accessed=2 * (weights.size + hidden.size + tokens * model_width),
            transcendentals=0,
        ),
        name="forward_parts",
    )(me, cols, hidden, weights)


def update_kernel(scale, shards, me_ref, cols_ref, hid_ref, w_ref, m_ref, mate_w_ref, mate_m_ref, *refs):
    own, others = refs[0], refs[1 : 2 * shards - 1]
    new_w_ref, new_m_ref, section, sem = refs[2 * shards - 1 :]
    step = pl.program_id(0)
    rows_step, block_size = w_ref.shape[0], w_ref.shape[1]
    per_row = w_ref.shape[2] // block_size
    me = me_ref[0]
    count = own.shape[0]

    def copy_in(source, shard, number):
        start = pl.multiple_of(shard * count, count)
        return pltpu.make_async_copy(source, section.at[pl.ds(start, count), :], sem.at[number])

    def for_each(act):
        act(copy_in(own, me, 0))
        for s in range(1, shards):

            @pl.when(me >= s)
            def _(s=s):
                act(copy_in(others[2 * s - 2], me - s, 2 * s - 1))

            @pl.when(me + s < shards)
            def _(s=s):
                act(copy_in(others[2 * s - 1], me + s, 2 * s))

    @pl.when(step == 0)
    def _():
        for_each(lambda c: c.start())
        for_each(lambda c: c.wait())

    for i in range(rows_step):
        hid = hid_ref[:, i * block_size : (i + 1) * block_size]
        for k in range(per_row):
            col = cols_ref[step * rows_step + i, k]
            selected = section[:, pl.ds(pl.multiple_of(col * block_size, block_size), block_size)]
            gradient = scale * lax.dot_general(
                hid, selected, (((0,), (0,)), ((), ())), preferred_element_type=jnp.float32
            )
            at = (i, slice(None), slice(k * block_size, (k + 1) * block_size))
            own_w = w_ref[at].astype(jnp.float32)
            mean_w = 0.5 * (own_w + mate_w_ref[at].astype(jnp.float32))
            mean_m = 0.5 * (m_ref[at].astype(jnp.float32) + mate_m_ref[at].astype(jnp.float32))
            corrected = gradient + LAMBDA_DC * gradient * gradient * (mean_w - own_w)
            moment = MOMENT_DECAY * mean_m + corrected
            new_m_ref[at] = moment.astype(jnp.bfloat16)
            new_w_ref[at] = (mean_w - LEARN_RATE * moment).astype(jnp.bfloat16)


def update(me, cols, hidden, weights, momentum, mate_w, mate_m, section, scale, shards):
    tokens = hidden.shape[0]
    row_blocks, block_size, width = weights.shape
    rows_step = 2 if row_blocks % 2 == 0 else 1
    model_width = section[0].shape[1]
    blocks = pl.BlockSpec((rows_step, block_size, width), lambda r, *_: (r, 0, 0))
    shape = jax.ShapeDtypeStruct(weights.shape, jnp.bfloat16)
    return pl.pallas_call(
        functools.partial(update_kernel, scale, shards),
        out_shape=[shape, shape],
        grid_spec=pltpu.PrefetchScalarGridSpec(
            num_scalar_prefetch=2,
            grid=(row_blocks // rows_step,),
            in_specs=[pl.BlockSpec((tokens, rows_step * block_size), lambda r, *_: (0, r))]
            + [blocks] * 4
            + [pl.BlockSpec(memory_space=pl.ANY)] * len(section),
            out_specs=[blocks, blocks],
            scratch_shapes=[
                pltpu.VMEM((tokens, model_width), jnp.bfloat16),
                pltpu.SemaphoreType.DMA((2 * shards - 1,)),
            ],
        ),
        compiler_params=pltpu.CompilerParams(vmem_limit_bytes=VMEM_LIMIT),
        cost_estimate=pl.CostEstimate(
            flops=2 * tokens * weights.size,
            bytes_accessed=2 * (6 * weights.size + hidden.size + tokens * model_width),
            transcendentals=0,
        ),
        name="update",
    )(me, cols, hidden, weights, momentum, mate_w, mate_m, *section)


def gather_chain(own, shards):
    arrived, up, down = [], own, own
    for s in range(1, shards):
        up = lax.ppermute(up, "tensor", [(i, i + 1) for i in range(s - 1, shards - 1)])
        down = lax.ppermute(down, "tensor", [(i, i - 1) for i in range(shards - s, 0, -1)])
        arrived += [up, down]
    return arrived


def scatter_chain(slots, shards):
    up = down = None
    for t in range(shards - 1):
        send_up, send_down = slots[shards - 1 - t], slots[t + 1]
        if t:
            send_up, send_down = send_up + up, send_down + down
        up = lax.ppermute(send_up, "tensor", [(i, i + 1) for i in range(t + 1)])
        down = lax.ppermute(send_down, "tensor", [(shards - 1 - i, shards - 2 - i) for i in range(t + 1)])
    total = slots[0].astype(jnp.float32) + up.astype(jnp.float32) + down.astype(jnp.float32)
    return total.astype(jnp.bfloat16)


def step_for(bit, hidden, out_grad, weights, momentum, cols):
    shards = lax.axis_size("tensor")
    replicas = lax.axis_size("replica")
    model_width = out_grad.shape[1]
    scale = (4.0 / (hidden.shape[1] * shards)) ** 0.5
    me = lax.axis_index("tensor").reshape(1).astype(jnp.int32)
    pairs = [(i, i ^ 1 << bit) for i in range(replicas)]
    mate_w = lax.ppermute(weights, "replica", pairs)
    mate_m = lax.ppermute(momentum, "replica", pairs)
    arrived = gather_chain(out_grad, shards)
    slots = forward_parts(me, cols, hidden, weights, scale, shards, model_width)
    outputs = scatter_chain(slots, shards)
    new_w, new_m = update(
        me, cols, hidden, weights, momentum, mate_w, mate_m, [out_grad, *arrived], scale, shards
    )
    return outputs, new_w, new_m


def body(hidden, out_grad, weights, momentum, block_cols, step_number):
    levels = lax.axis_size("replica").bit_length() - 1
    outputs, new_w, new_m = lax.switch(
        lax.rem(step_number[0], levels),
        [functools.partial(step_for, bit) for bit in range(levels)],
        hidden,
        out_grad,
        weights[0],
        momentum[0],
        block_cols,
    )
    return outputs, new_w[None], new_m[None]


def solution(mesh):
    return jax.shard_map(
        body,
        mesh=mesh,
        in_specs=(
            P("replica", "tensor"),
            P(("replica", "tensor"), None),
            P("replica", "tensor", None, None),
            P("replica", "tensor", None, None),
            P("tensor", None),
            P(),
        ),
        out_specs=(
            P(("replica", "tensor"), None),
            P("replica", "tensor", None, None),
            P("replica", "tensor", None, None),
        ),
        check_vma=False,
    )
```

time: 131 us -> 176 us (1.34)
  waiting for transfers between devices: 1.06 us -> 119 us
  local copies, waits for them, and re-layouts: 70.2 us -> 1.58 us
  matrix products: 42.4 us -> 0 us
  starting transfers between devices: 0.59 us -> 32.8 us
  Pallas kernels: 0 us -> 19.8 us
  between operations: 14.7 us -> 1.3 us
    ppermute x2 -> x14, waiting for transfers between devices: 0.36 us -> 119 us  [the longest x1 74.9 us: step_for(): mate_m = lax.ppermute(momentum, 'replica', pairs)]
    dot_general x4 -> x0, matrix products: 42.4 us -> none  [the longest x1 16.6 us: body(): jnp.dot(hid_rows, dense_w, preferred_element_type=jnp.float32)]
    unnamed x11 -> x10, local copies, waits for them, and re-layouts: 34.8 us -> 0.81 us
    ppermute x2 -> x14, starting transfers between devices: 0.51 us -> 32.8 us  [the longest x3 20.4 us: scatter_chain(): up = lax.ppermute(send_up, 'tensor', [(i, i + 1) for i in range(t + 1)])]
    another operation x4 -> x1, local copies, waits for them, and re-layouts: 24.3 us -> 0.77 us
    pallas_call x0 -> x2, Pallas kernels: none -> 19.8 us  [the longest x1 12 us: update(): pl.pallas_call(functools.partial(update_kernel, scale, shards), out_shape...]
    reshape x1 -> x0, local copies, waits for them, and re-layouts: 11 us -> none  [body(): selected = selected.reshape(row_blocks, row_count, per_row * block_size)]
  transfers between devices with their start and end apart: 4 -> 14, of which waited for: 1 -> 7; matrix products, arithmetic and copies ran while one was open for 87% -> 1% of each run, Pallas kernels for 0% -> 4%
where the time goes in v1:
time: 176 us
  waiting for transfers between devices  119 us (68%)
  starting transfers between devices  32.8 us (19%)
  Pallas kernels  19.8 us (11%)
    ppermute x1, waiting for transfers between devices, step_for(): mate_m = lax.ppermute(momentum, 'replica', pairs)  74.9 us
    ppermute x3, starting transfers between devices, scatter_chain(): up = lax.ppermute(send_up, 'tensor', [(i, i + 1) for i in range(t + 1)])  20.4 us
    ppermute x3, waiting for transfers between devices, scatter_chain(): up = lax.ppermute(send_up, 'tensor', [(i, i + 1) for i in range(t + 1)])  17.9 us
    ppermute x3, waiting for transfers between devices, gather_chain(): lax.ppermute(down, 'tensor', [(i, i - 1) for i in range(shards - s, 0, -1)])  13.4 us
    pallas_call x1, Pallas kernels, update(): pl.pallas_call(functools.partial(update_kernel, scale, shards), out_shape...  12 us
    pallas_call x1, Pallas kernels, forward_parts(): pl.pallas_call(functools.partial(forward_kernel, scale, shards), out_shap...  7.82 us
    ppermute x3, waiting for transfers between devices, gather_chain(): lax.ppermute(up, 'tensor', [(i, i + 1) for i in range(s - 1, shards - 1)])  7.22 us
    ppermute x3, waiting for transfers between devices, scatter_chain(): lax.ppermute(send_down, 'tensor', [(shards - 1 - i, shards - 2 - i) for i...  5.79 us
  transfers between devices with their start and end apart: 14, of which 7 were waited for; matrix products, arithmetic and copies ran while one was open for 1% of the time, Pallas kernels for 4%

profile of v1, /device:TPU:0, one launch (start us, length us, event | category | flops | bytes accessed | tf_op | source)
XLA Modules:
  0.0 175.7 jit_solution(140149861402562655)
XLA Ops:
  1.3 173.6 %conditional.4 = (bf16[14,128,1024]{2,1,0:T(8,128)(2,1)}, bf16[14,128,1024]{2,1,0:T(8,128)(2,1)}, bf16[64,4096]{1,0:T(8,128)(2,1)S(1)}) conditional(s32[]{:T(128)} %bitcast.3, (bf16[14,128,1024]{2,1,0:T(8,128)(2,1)}, bf16[14,128,1024]{2,1,0:T(8,128)(2,1)}, bf16[64,4096]{1,0:T(8,128)(2,1)}, s32[14,8]{0,1:T(8,128)}, ...), branch_computations={%region_0.0_spmd, %region_1.0_spmd, %region_2.0_spmd} | conditional | flops 1881669632 | bytes 129238600
  1.3 0.0 copy-start.10
  1.3 3.0 %collective-permute-start.14 = (bf16[14,128,1024]{2,1,0:T(8,128)(2,1)}, bf16[14,128,1024]{2,1,0:T(8,128)(2,1)}, u32[]{:S(2)}, u32[]{:S(2)}) collective-permute-start(bf16[14,128,1024]{2,1,0:T(8,128)(2,1)} %get-tuple-element.53.w_ref), channel_id=1, source_target_pairs={{0,8},{4,12},{8,0},{12,4},{16,24},{20,28},{24,16},{28,20},{1,9},{5... | collective-permute-start | bytes 11010056 | tf_op jit(solution)/shard_map/cond/branch_1_fun/ppermute | solution.py:182
  4.3 0.1 collective-permute-start.15
  4.4 0.8 copy.10.cols_ref
  5.2 7.8 %forward_parts.4 = (bf16[64,4096]{1,0:T(8,128)(2,1)S(1)}, bf16[64,4096]{1,0:T(8,128)(2,1)S(1)}, bf16[64,4096]{1,0:T(8,128)(2,1)S(1)}, bf16[64,4096]{1,0:T(8,128)(2,1)S(1)}) custom-call(s32[1]{0:T(128)} %bitcast.1.me_ref, s32[14,8]{1,0:T(8,128)S(1)} %copy.10.cols_ref, bf16[256,1792]{1,0:T(8,128)(2,1)} %get-tuple-element.52.hid_ref, ...), custom_call_target="tpu_custom_call" | custom-call | flops 939524096 | bytes 6684672 | tf_op jit(solution)/shard_map/cond/branch_1_fun/forward_parts/pallas_call | solution.py:51
  13.0 4.0 %collective-permute-start.22 = (bf16[64,4096]{1,0:T(8,128)(2,1)S(1)}, bf16[64,4096]{1,0:T(8,128)(2,1)S(1)}, u32[]{:S(2)}, u32[]{:S(2)}) collective-permute-start(bf16[64,4096]{1,0:T(8,128)(2,1)S(1)} %get-tuple-element.61), channel_id=1, source_target_pairs={{0,1},{4,5},{8,9},{12,13},{16,17},{20,21},{24,25},{28,29}} | collective-permute-start | bytes 1572872 | tf_op jit(solution)/shard_map/cond/branch_1_fun/ppermute | solution.py:169
  17.0 0.7 collective-permute-start.25
  17.7 1.3 collective-permute-start.16
  19.0 10.3 %collective-permute-done.22 = bf16[64,4096]{1,0:T(8,128)(2,1)S(1)} collective-permute-done((bf16[64,4096]{1,0:T(8,128)(2,1)S(1)}, bf16[64,4096]{1,0:T(8,128)(2,1)S(1)}, u32[]{:S(2)}, u32[]{:S(2)}) %collective-permute-start.22) | collective-permute-done | bytes 524320 | tf_op jit(solution)/shard_map/cond/branch_1_fun/ppermute | solution.py:169
  29.3 1.3 collective-permute-start.17
  30.6 0.1 fusion.1
  30.7 0.8 collective-permute-start.26
  31.6 7.2 %collective-permute-done.16.refs_1_ = bf16[64,4096]{1,0:T(8,128)(2,1)S(1)} collective-permute-done((bf16[64,4096]{1,0:T(8,128)(2,1)S(1)}, bf16[64,4096]{1,0:T(8,128)(2,1)S(1)}, u32[]{:S(2)}, u32[]{:S(2)}) %collective-permute-start.16) | collective-permute-done | bytes 524320 | tf_op jit(solution)/shard_map/cond/branch_1_fun/ppermute | solution.py:157
  38.8 4.4 %collective-permute-start.23 = (bf16[64,4096]{1,0:T(8,128)(2,1)S(1)}, bf16[64,4096]{1,0:T(8,128)(2,1)S(1)}, u32[]{:S(2)}, u32[]{:S(2)}) collective-permute-start(bf16[64,4096]{1,0:T(8,128)(2,1)S(1)} %get-tuple-element.104), channel_id=1, source_target_pairs={{0,1},{1,2},{4,5},{5,6},{8,9},{9,10},{12,13},{13,14},{16,17},{17,1... | collective-permute-start | bytes 1572872 | tf_op jit(solution)/shard_map/cond/branch_1_fun/ppermute | solution.py:169
  43.2 0.7 collective-permute-start.18
  43.9 1.3 collective-permute-start.19
  45.2 0.1 add.46
  45.4 7.6 %collective-permute-done.23 = bf16[64,4096]{1,0:T(8,128)(2,1)S(1)} collective-permute-done((bf16[64,4096]{1,0:T(8,128)(2,1)S(1)}, bf16[64,4096]{1,0:T(8,128)(2,1)S(1)}, u32[]{:S(2)}, u32[]{:S(2)}) %collective-permute-start.23) | collective-permute-done | bytes 524320 | tf_op jit(solution)/shard_map/cond/branch_1_fun/ppermute | solution.py:169
  53.0 1.3 collective-permute-start.27
  54.2 0.1 add.43
  54.4 12.0 %collective-permute-start.24 = (bf16[64,4096]{1,0:T(8,128)(2,1)S(1)}, bf16[64,4096]{1,0:T(8,128)(2,1)S(1)}, u32[]{:S(2)}, u32[]{:S(2)}) collective-permute-start(bf16[64,4096]{1,0:T(8,128)(2,1)S(1)} %add.43), channel_id=1, source_target_pairs={{0,1},{1,2},{2,3},{4,5},{5,6},{6,7},{8,9},{9,10},{10,11},{12,13},{... | collective-permute-start | bytes 1572872 | tf_op jit(solution)/shard_map/cond/branch_1_fun/ppermute | solution.py:169
  66.4 3.8 %collective-permute-done.19.refs_4_ = bf16[64,4096]{1,0:T(8,128)(2,1)S(1)} collective-permute-done((bf16[64,4096]{1,0:T(8,128)(2,1)S(1)}, bf16[64,4096]{1,0:T(8,128)(2,1)S(1)}, u32[]{:S(2)}, u32[]{:S(2)}) %collective-permute-start.19) | collective-permute-done | bytes 524320 | tf_op jit(solution)/shard_map/cond/branch_1_fun/ppermute | solution.py:158
  70.2 0.7 collective-permute-start.20
  70.9 5.8 %collective-permute-done.27 = bf16[64,4096]{1,0:T(8,128)(2,1)S(1)} collective-permute-done((bf16[64,4096]{1,0:T(8,128)(2,1)S(1)}, bf16[64,4096]{1,0:T(8,128)(2,1)S(1)}, u32[]{:S(2)}, u32[]{:S(2)}) %collective-permute-start.27) | collective-permute-done | bytes 524320 | tf_op jit(solution)/shard_map/cond/branch_1_fun/ppermute | solution.py:170
  76.6 1.3 collective-permute-start.21
  77.9 0.2 add_convert_fusion.1
  78.1 9.6 %collective-permute-done.21.refs_6_ = bf16[64,4096]{1,0:T(8,128)(2,1)S(1)} collective-permute-done((bf16[64,4096]{1,0:T(8,128)(2,1)S(1)}, bf16[64,4096]{1,0:T(8,128)(2,1)S(1)}, u32[]{:S(2)}, u32[]{:S(2)}) %collective-permute-start.21) | collective-permute-done | bytes 524320 | tf_op jit(solution)/shard_map/cond/branch_1_fun/ppermute | solution.py:158
  87.8 74.9 %collective-permute-done.15.mate_m_ref = bf16[14,128,1024]{2,1,0:T(8,128)(2,1)} collective-permute-done((bf16[14,128,1024]{2,1,0:T(8,128)(2,1)}, bf16[14,128,1024]{2,1,0:T(8,128)(2,1)}, u32[]{:S(2)}, u32[]{:S(2)}) %collective-permute-start.15) | collective-permute-done | bytes 3670048 | tf_op jit(solution)/shard_map/cond/branch_1_fun/ppermute | solution.py:183
  162.6 12.0 %update.4 = (bf16[14,128,1024]{2,1,0:T(8,128)(2,1)}, bf16[14,128,1024]{2,1,0:T(8,128)(2,1)}) custom-call(s32[1]{0:T(128)} %bitcast.1.me_ref, s32[14,8]{1,0:T(8,128)S(1)} %copy.10.cols_ref, bf16[256,1792]{1,0:T(8,128)(2,1)S(1)} %copy-done.7, bf16[14,128,1024]{2,1,0:T(8,128)(2,1)S(1)} %copy-done.1, bf16[14,128,1024]{2,1,0:T(8,128)(2,1)S(1)} %copy-done.4, ...), custom_call_target="tpu_custom_call" | custom-call | flops 939524096 | bytes 25034752 | tf_op jit(solution)/shard_map/cond/branch_1_fun/update/pallas_call | solution.py:129
  174.9 0.0 copy-start.12
  174.9 0.8 copy-done.12
  (14 shorter events, 0.0 us)
Async XLA Ops:
  1.3 16.4 %copy-start.10 = (bf16[64,4096]{1,0:T(8,128)(2,1)S(1)}, bf16[64,4096]{1,0:T(8,128)(2,1)}, u32[]{:S(2)}) copy-start(bf16[64,4096]{1,0:T(8,128)(2,1)} %get-tuple-element.55.refs_0_) | copy-start | bytes 1572868
  1.3 86.4 %collective-permute-start.14 = (bf16[14,128,1024]{2,1,0:T(8,128)(2,1)}, bf16[14,128,1024]{2,1,0:T(8,128)(2,1)}, u32[]{:S(2)}, u32[]{:S(2)}) collective-permute-start(bf16[14,128,1024]{2,1,0:T(8,128)(2,1)} %get-tuple-element.53.w_ref), channel_id=1, source_target_pairs={{0,8},{4,12},{8,0},{12,4},{16,24},{20,28},{24,16},{28,20},{1,9},{5... | collective-permute-start | bytes 11010056 | tf_op jit(solution)/shard_map/cond/branch_1_fun/ppermute | solution.py:182
  4.3 158.3 %collective-permute-start.15 = (bf16[14,128,1024]{2,1,0:T(8,128)(2,1)}, bf16[14,128,1024]{2,1,0:T(8,128)(2,1)}, u32[]{:S(2)}, u32[]{:S(2)}) collective-permute-start(bf16[14,128,1024]{2,1,0:T(8,128)(2,1)} %get-tuple-element.54.m_ref), channel_id=1, source_target_pairs={{0,8},{4,12},{8,0},{12,4},{16,24},{20,28},{24,16},{28,20},{1,9},{5... | collective-permute-start | bytes 11010056 | tf_op jit(solution)/shard_map/cond/branch_1_fun/ppermute | solution.py:183
  5.2 157.5 %copy-start.7 = (bf16[256,1792]{1,0:T(8,128)(2,1)S(1)}, bf16[256,1792]{1,0:T(8,128)(2,1)}, u32[]{:S(2)}) copy-start(bf16[256,1792]{1,0:T(8,128)(2,1)} %get-tuple-element.52.hid_ref) | copy-start | bytes 2752516
  13.0 16.3 %collective-permute-start.22 = (bf16[64,4096]{1,0:T(8,128)(2,1)S(1)}, bf16[64,4096]{1,0:T(8,128)(2,1)S(1)}, u32[]{:S(2)}, u32[]{:S(2)}) collective-permute-start(bf16[64,4096]{1,0:T(8,128)(2,1)S(1)} %get-tuple-element.61), channel_id=1, source_target_pairs={{0,1},{4,5},{8,9},{12,13},{16,17},{20,21},{24,25},{28,29}} | collective-permute-start | bytes 1572872 | tf_op jit(solution)/shard_map/cond/branch_1_fun/ppermute | solution.py:169
  17.0 13.6 %collective-permute-start.25 = (bf16[64,4096]{1,0:T(8,128)(2,1)S(1)}, bf16[64,4096]{1,0:T(8,128)(2,1)S(1)}, u32[]{:S(2)}, u32[]{:S(2)}) collective-permute-start(bf16[64,4096]{1,0:T(8,128)(2,1)S(1)} %get-tuple-element.59), channel_id=1, source_target_pairs={{3,2},{7,6},{11,10},{15,14},{19,18},{23,22},{27,26},{31,30}} | collective-permute-start | bytes 1572872 | tf_op jit(solution)/shard_map/cond/branch_1_fun/ppermute | solution.py:170
  17.7 21.1 %collective-permute-start.16 = (bf16[64,4096]{1,0:T(8,128)(2,1)S(1)}, bf16[64,4096]{1,0:T(8,128)(2,1)S(1)}, u32[]{:S(2)}, u32[]{:S(2)}) collective-permute-start(bf16[64,4096]{1,0:T(8,128)(2,1)S(1)} %copy-done.10), channel_id=1, source_target_pairs={{0,1},{1,2},{2,3},{4,5},{5,6},{6,7},{8,9},{9,10},{10,11},{12,13},{... | collective-permute-start | bytes 1572872 | tf_op jit(solution)/shard_map/cond/branch_1_fun/ppermute | solution.py:157
  29.3 13.9 %collective-permute-start.17 = (bf16[64,4096]{1,0:T(8,128)(2,1)S(1)}, bf16[64,4096]{1,0:T(8,128)(2,1)S(1)}, u32[]{:S(2)}, u32[]{:S(2)}) collective-permute-start(bf16[64,4096]{1,0:T(8,128)(2,1)S(1)} %copy-done.10), channel_id=1, source_target_pairs={{3,2},{2,1},{1,0},{7,6},{6,5},{5,4},{11,10},{10,9},{9,8},{15,14},{... | collective-permute-start | bytes 1572872 | tf_op jit(solution)/shard_map/cond/branch_1_fun/ppermute | solution.py:158
  30.6 132.0 %copy-start.1 = (bf16[14,128,1024]{2,1,0:T(8,128)(2,1)S(1)}, bf16[14,128,1024]{2,1,0:T(8,128)(2,1)}, u32[]{:S(2)}) copy-start(bf16[14,128,1024]{2,1,0:T(8,128)(2,1)} %get-tuple-element.53.w_ref) | copy-start | bytes 11010052
  30.6 132.0 %copy-start.4 = (bf16[14,128,1024]{2,1,0:T(8,128)(2,1)S(1)}, bf16[14,128,1024]{2,1,0:T(8,128)(2,1)}, u32[]{:S(2)}) copy-start(bf16[14,128,1024]{2,1,0:T(8,128)(2,1)} %get-tuple-element.54.m_ref) | copy-start | bytes 11010052
  30.7 13.2 %collective-permute-start.26 = (bf16[64,4096]{1,0:T(8,128)(2,1)S(1)}, bf16[64,4096]{1,0:T(8,128)(2,1)S(1)}, u32[]{:S(2)}, u32[]{:S(2)}) collective-permute-start(bf16[64,4096]{1,0:T(8,128)(2,1)S(1)} %get-tuple-element.105), channel_id=1, source_target_pairs={{3,2},{2,1},{7,6},{6,5},{11,10},{10,9},{15,14},{14,13},{19,18},{18... | collective-permute-start | bytes 1572872 | tf_op jit(solution)/shard_map/cond/branch_1_fun/ppermute | solution.py:170
  38.8 14.2 %collective-permute-start.23 = (bf16[64,4096]{1,0:T(8,128)(2,1)S(1)}, bf16[64,4096]{1,0:T(8,128)(2,1)S(1)}, u32[]{:S(2)}, u32[]{:S(2)}) collective-permute-start(bf16[64,4096]{1,0:T(8,128)(2,1)S(1)} %get-tuple-element.104), channel_id=1, source_target_pairs={{0,1},{1,2},{4,5},{5,6},{8,9},{9,10},{12,13},{13,14},{16,17},{17,1... | collective-permute-start | bytes 1572872 | tf_op jit(solution)/shard_map/cond/branch_1_fun/ppermute | solution.py:169
  43.2 11.2 %collective-permute-start.18 = (bf16[64,4096]{1,0:T(8,128)(2,1)S(1)}, bf16[64,4096]{1,0:T(8,128)(2,1)S(1)}, u32[]{:S(2)}, u32[]{:S(2)}) collective-permute-start(bf16[64,4096]{1,0:T(8,128)(2,1)S(1)} %collective-permute-done.16.refs_1_), channel_id=1, source_target_pairs={{1,2},{2,3},{5,6},{6,7},{9,10},{10,11},{13,14},{14,15},{17,18},{18... | collective-permute-start | bytes 1572872 | tf_op jit(solution)/shard_map/cond/branch_1_fun/ppermute | solution.py:157
  43.9 26.2 %collective-permute-start.19 = (bf16[64,4096]{1,0:T(8,128)(2,1)S(1)}, bf16[64,4096]{1,0:T(8,128)(2,1)S(1)}, u32[]{:S(2)}, u32[]{:S(2)}) collective-permute-start(bf16[64,4096]{1,0:T(8,128)(2,1)S(1)} %collective-permute-done.17.refs_2_), channel_id=1, source_target_pairs={{2,1},{1,0},{6,5},{5,4},{10,9},{9,8},{14,13},{13,12},{18,17},{17,1... | collective-permute-start | bytes 1572872 | tf_op jit(solution)/shard_map/cond/branch_1_fun/ppermute | solution.py:158
  53.0 23.7 %collective-permute-start.27 = (bf16[64,4096]{1,0:T(8,128)(2,1)S(1)}, bf16[64,4096]{1,0:T(8,128)(2,1)S(1)}, u32[]{:S(2)}, u32[]{:S(2)}) collective-permute-start(bf16[64,4096]{1,0:T(8,128)(2,1)S(1)} %add.46), channel_id=1, source_target_pairs={{3,2},{2,1},{1,0},{7,6},{6,5},{5,4},{11,10},{10,9},{9,8},{15,14},{... | collective-permute-start | bytes 1572872 | tf_op jit(solution)/shard_map/cond/branch_1_fun/ppermute | solution.py:170
  54.4 23.5 %collective-permute-start.24 = (bf16[64,4096]{1,0:T(8,128)(2,1)S(1)}, bf16[64,4096]{1,0:T(8,128)(2,1)S(1)}, u32[]{:S(2)}, u32[]{:S(2)}) collective-permute-start(bf16[64,4096]{1,0:T(8,128)(2,1)S(1)} %add.43), channel_id=1, source_target_pairs={{0,1},{1,2},{2,3},{4,5},{5,6},{6,7},{8,9},{9,10},{10,11},{12,13},{... | collective-permute-start | bytes 1572872 | tf_op jit(solution)/shard_map/cond/branch_1_fun/ppermute | solution.py:169
  70.2 8.0 %collective-permute-start.20 = (bf16[64,4096]{1,0:T(8,128)(2,1)S(1)}, bf16[64,4096]{1,0:T(8,128)(2,1)S(1)}, u32[]{:S(2)}, u32[]{:S(2)}) collective-permute-start(bf16[64,4096]{1,0:T(8,128)(2,1)S(1)} %collective-permute-done.18.refs_3_), channel_id=1, source_target_pairs={{2,3},{6,7},{10,11},{14,15},{18,19},{22,23},{26,27},{30,31}} | collective-permute-start | bytes 1572872 | tf_op jit(solution)/shard_map/cond/branch_1_fun/ppermute | solution.py:157
  76.6 11.1 %collective-permute-start.21 = (bf16[64,4096]{1,0:T(8,128)(2,1)S(1)}, bf16[64,4096]{1,0:T(8,128)(2,1)S(1)}, u32[]{:S(2)}, u32[]{:S(2)}) collective-permute-start(bf16[64,4096]{1,0:T(8,128)(2,1)S(1)} %collective-permute-done.19.refs_4_), channel_id=1, source_target_pairs={{1,0},{5,4},{9,8},{13,12},{17,16},{21,20},{25,24},{29,28}} | collective-permute-start | bytes 1572872 | tf_op jit(solution)/shard_map/cond/branch_1_fun/ppermute | solution.py:158
  174.9 0.8 copy-start.12

commit v2 on v1

v2 whole, which is shorter than its diff:
```python
import functools

import jax
import jax.numpy as jnp
from jax import lax
from jax.experimental import pallas as pl
from jax.experimental.pallas import tpu as pltpu
from jax.sharding import PartitionSpec as P

LAMBDA_DC = 1.0
MOMENT_DECAY = 0.9
LEARN_RATE = 0.2
VMEM_LIMIT = 14 * 1024 * 1024
LIGHT = pl.CostEstimate(flops=1024, bytes_accessed=1024, transcendentals=0)
ANYWHERE = pl.BlockSpec(memory_space=pl.ANY)
IN_VMEM = pl.BlockSpec(memory_space=pltpu.VMEM)


def rows_per_step(row_blocks):
    return 2 if row_blocks % 2 == 0 else 1


def forward_kernel(scale, shards, pieces, me_ref, cols_ref, hid_ref, w_ref, *refs):
    parts, total = refs[:-1], refs[-1]
    step = pl.program_id(0)
    rows_step, block_size = w_ref.shape[0], w_ref.shape[1]
    per_row = w_ref.shape[2] // block_size

    @pl.when(step == 0)
    def _():
        total[...] = jnp.zeros_like(total)

    for i in range(rows_step):
        product = jnp.dot(
            hid_ref[:, i * block_size : (i + 1) * block_size],
            w_ref[i],
            preferred_element_type=jnp.float32,
        )
        for k in range(per_row):
            col = cols_ref[k, step * rows_step + i]
            total[col] += product[:, k * block_size : (k + 1) * block_size]

    @pl.when(step == pl.num_programs(0) - 1)
    def _():
        me = me_ref[0]
        even = lax.rem(me, 2) == 0
        below, above = jnp.where(even, me, shards - 1 - me), jnp.where(even, shards - 1 - me, me)
        ahead = jnp.where(even, 1, -1)
        kept = [(me, None)]
        for p in range(1, shards):
            kept += [(me + ahead * (shards - p), below <= p - 1), (me - ahead * (shards - p), above <= p - 1)]
        rows = parts[0].shape[0]
        for number, part in enumerate(parts):
            owner, used = kept[number // pieces]
            factor = scale if used is None else jnp.where(used, scale, 0.0)
            place = jnp.clip(owner, 0, shards - 1) * pieces + number % pieces
            start = pl.multiple_of(place * rows, rows)
            for col in range(total.shape[0]):
                value = total[col, pl.ds(start, rows), :] * factor
                part[:, col * block_size : (col + 1) * block_size] = value.astype(jnp.bfloat16)


def forward_parts(me, cols, hidden, weights, scale, shards, pieces, model_width):
    tokens = hidden.shape[0]
    row_blocks, block_size, width = weights.shape
    rows_step = rows_per_step(row_blocks)
    rows = tokens // shards // pieces
    count = pieces * (2 * shards - 1)
    return pl.pallas_call(
        functools.partial(forward_kernel, scale, shards, pieces),
        out_shape=[jax.ShapeDtypeStruct((rows, model_width), jnp.bfloat16)] * count,
        grid_spec=pltpu.PrefetchScalarGridSpec(
            num_scalar_prefetch=2,
            grid=(row_blocks // rows_step,),
            in_specs=[
                pl.BlockSpec((tokens, rows_step * block_size), lambda r, *_: (0, r)),
                pl.BlockSpec((rows_step, block_size, width), lambda r, *_: (r, 0, 0)),
            ],
            out_specs=[pl.BlockSpec((rows, model_width), lambda r, *_: (0, 0))] * count,
            scratch_shapes=[pltpu.VMEM((model_width // block_size, tokens, block_size), jnp.float32)],
        ),
        compiler_params=pltpu.CompilerParams(vmem_limit_bytes=VMEM_LIMIT),
        cost_estimate=LIGHT,
        name="forward_parts",
    )(me, cols, hidden, weights)


def put_shards(me, shards, given, section, sem):
    ahead = 1 - 2 * lax.rem(me, 2)
    for act in ("start", "wait"):
        for number, (step, side, piece, pieces, ref) in enumerate(given):
            shard = me + ahead * (step if side == 0 else -step)
            rows = ref.shape[0]

            @pl.when((shard >= 0) & (shard < shards))
            def _(act=act, number=number, piece=piece, pieces=pieces, ref=ref, shard=shard, rows=rows):
                to = section.at[pl.ds(pl.multiple_of((shard * pieces + piece) * rows, rows), rows), :]
                getattr(pltpu.make_async_copy(ref, to, sem.at[number]), act)()


def section_kernel(shards, labels, me_ref, *refs):
    section, sem = refs[-2:]
    put_shards(me_ref[0], shards, [(*a, r) for a, r in zip(labels, refs)], section, sem)


def start_section(me, shards, given):
    labels, arrays = [a for a, _ in given], [a for _, a in given]
    rows, width = arrays[0].shape
    return pl.pallas_call(
        functools.partial(section_kernel, shards, labels),
        out_shape=jax.ShapeDtypeStruct((rows * labels[0][3] * shards, width), jnp.bfloat16),
        grid_spec=pltpu.PrefetchScalarGridSpec(
            num_scalar_prefetch=1,
            grid=(),
            in_specs=[ANYWHERE] * len(arrays),
            out_specs=IN_VMEM,
            scratch_shapes=[pltpu.SemaphoreType.DMA((len(arrays),))],
        ),
        compiler_params=pltpu.CompilerParams(vmem_limit_bytes=VMEM_LIMIT),
        cost_estimate=LIGHT,
        name="start_section",
    )(me, *arrays)


def update_kernel(scale, shards, first, count, labels, me_ref, cols_ref, hid_ref, w_ref, m_ref, mate_w_ref, mate_m_ref, section, *refs):
    late, (held_w, held_m, sem) = refs[: len(labels)], refs[-3:]
    new_w_ref, new_m_ref = refs[-6:-4] if labels else refs[-5:-3]
    block_size = w_ref.shape[1]
    per_row = w_ref.shape[2] // block_size
    if labels:
        section = refs[-4]
        put_shards(me_ref[0], shards, [(*a, r) for a, r in zip(labels, late)], section, sem.at[2])

    def copies_out(i):
        return [
            pltpu.make_async_copy(held.at[i], new.at[first + i], sem.at[number, i])
            for number, (held, new) in enumerate(((held_w, new_w_ref), (held_m, new_m_ref)))
        ]

    for i in range(count):
        hid = hid_ref[:, i * block_size : (i + 1) * block_size].T
        for k in range(0, per_row, 2):
            selected = []
            for j in range(2):
                col = cols_ref[k + j, first + i]
                selected.append(section[:, pl.ds(pl.multiple_of(col * block_size, block_size), block_size)])
            gradient = scale * jnp.dot(hid, jnp.concatenate(selected, 1), preferred_element_type=jnp.float32)
            at = (slice(None), slice(k * block_size, (k + 2) * block_size))
            own_w, mate_w = w_ref[i, *at], mate_w_ref[i, *at]
            half_gap = 0.5 * (mate_w - own_w).astype(jnp.float32)
            mean_w = 0.5 * (own_w + mate_w).astype(jnp.float32)
            corrected = gradient + LAMBDA_DC * gradient * gradient * half_gap
            moment = (0.5 * MOMENT_DECAY) * (m_ref[i, *at] + mate_m_ref[i, *at]).astype(jnp.float32) + corrected
            held_m[i, *at] = moment.astype(jnp.bfloat16)
            held_w[i, *at] = (mean_w - LEARN_RATE * moment).astype(jnp.bfloat16)
        for copy in copies_out(i):
            copy.start()
    for i in range(count):
        for copy in copies_out(i):
            copy.wait()


def update(me, cols, hidden, weights, momentum, mate_w, mate_m, section, late, scale, shards, first, made):
    count, block_size, width = mate_w.shape
    shape = jax.ShapeDtypeStruct(weights.shape, jnp.bfloat16)
    labels, arrays = [a for a, _ in late], [a for _, a in late]
    aliases = {8 + len(arrays) + i: i for i in range(len(made))}
    if late:
        aliases[7] = 2
    held = pltpu.VMEM((count, block_size, width), jnp.bfloat16)
    window = pl.BlockSpec((count, block_size, width), lambda i, *_: (first // count, 0, 0))
    whole = pl.BlockSpec(mate_w.shape, lambda i, *_: (0, 0, 0))
    hid = pl.BlockSpec((hidden.shape[0], count * block_size), lambda i, *_: (0, first // count))
    new = pl.pallas_call(
        functools.partial(update_kernel, scale, shards, first, count, labels),
        out_shape=[shape, shape] + [jax.ShapeDtypeStruct(section.shape, section.dtype)] * bool(late),
        grid_spec=pltpu.PrefetchScalarGridSpec(
            num_scalar_prefetch=2,
            grid=(1,),
            in_specs=[hid, window, window, whole, window, IN_VMEM] + [ANYWHERE] * (len(arrays) + len(made)),
            out_specs=[ANYWHERE, ANYWHERE] + [IN_VMEM] * bool(late),
            scratch_shapes=[held, held, pltpu.SemaphoreType.DMA((3, max(count, len(arrays))))],
        ),
        input_output_aliases=aliases,
        compiler_params=pltpu.CompilerParams(vmem_limit_bytes=VMEM_LIMIT),
        cost_estimate=LIGHT,
        name="update",
    )(me, cols, hidden, weights, momentum, mate_w, mate_m, section, *arrays, *made)
    return new[:2]


def add_kernel(*refs):
    (*terms, total, held, sem) = refs
    rows = terms[0].shape[0]
    for h in range(len(terms) // 3):
        for r in range(0, rows, 16):
            values = [t[r : r + 16, :].astype(jnp.float32) for t in terms[3 * h : 3 * h + 3]]
            held[h * rows + r : h * rows + r + 16, :] = sum(values).astype(jnp.bfloat16)
    copy = pltpu.make_async_copy(held, total, sem)
    copy.start()
    copy.wait()


def add_up(pieces):
    rows, width = pieces[0][0].shape
    shape = (rows * len(pieces), width)
    return pl.pallas_call(
        add_kernel,
        out_shape=jax.ShapeDtypeStruct(shape, jnp.bfloat16),
        in_specs=[IN_VMEM] * (3 * len(pieces)),
        out_specs=pl.BlockSpec(memory_space=pltpu.HBM),
        scratch_shapes=[pltpu.VMEM(shape, jnp.bfloat16), pltpu.SemaphoreType.DMA],
        compiler_params=pltpu.CompilerParams(vmem_limit_bytes=VMEM_LIMIT),
        cost_estimate=LIGHT,
        name="add_up",
    )(*[a for piece in pieces for a in piece])


def exchange(value, parity, shards):
    pairs = [(i, i + 1) for i in range(parity, shards - 1, 2)]
    return lax.ppermute(value, "tensor", pairs + [(j, i) for i, j in pairs])


def gather_and_scatter(own, make_parts, after_phase, along, shards, pieces):
    rows = own.shape[0] // pieces
    given, got = [((0, 0, 0, 1), own)], []
    for h in range(pieces):
        piece = own[h * rows : (h + 1) * rows]
        got.append([exchange(piece, side, shards) for side in (0, 1)])
    parts = make_parts()
    for p in range(1, shards):
        for h in range(pieces):
            got[h], parts, along[p - 1] = lax.optimization_barrier((got[h], parts, along[p - 1]))
            given += [((p, side, h, pieces), got[h][side]) for side in (0, 1)]
            part = [parts[(2 * p - 1 + side) * pieces + h] for side in (0, 1)]
            got[h] = [exchange(got[h][1 - side] + part[side], side, shards) for side in (0, 1)]
        if p == shards - 1 and pieces > 1:
            label, last = given[-1]
            last, got[:-1] = lax.optimization_barrier((last, got[:-1]))
            given[-1] = (label, last)
        result = after_phase(p, given, parts)
    result, along[shards - 1], got = lax.optimization_barrier((result, along[shards - 1], got))
    return result, add_up([(parts[h], *got[h]) for h in range(pieces)])


def step_for(bit, hidden, out_grad, weights, momentum, block_cols):
    shards = lax.axis_size("tensor")
    replicas = lax.axis_size("replica")
    model_width = out_grad.shape[1]
    scale = (4.0 / (hidden.shape[1] * shards)) ** 0.5
    me = lax.axis_index("tensor").reshape(1).astype(jnp.int32)
    cols = block_cols.T
    row_blocks = weights.shape[0]
    fixed = (me, cols, hidden, weights, momentum)

    def swap(value):
        return lax.ppermute(value, "replica", [(i, i ^ 1 << bit) for i in range(replicas)])

    def forward(pieces):
        return lambda: forward_parts(me, cols, hidden, weights, scale, shards, pieces, model_width)

    along = [[] for _ in range(shards)]
    along[0].append(swap(momentum))
    if bit == 0:
        counted = []

        def beside(p, given, parts):
            if p == 1:
                behind, _ = lax.optimization_barrier((weights, parts[0]))
                along[1].append(swap(behind))
            if p == shards - 2:
                counted.append(len(given))
                along[p].append(start_section(me, shards, given))
            if p == shards - 1:
                (mate_m,), (mate_w,) = along[:2]
                (section,), (count,) = along[p - 1], counted
                return update(*fixed, mate_w, mate_m, section, given[count:], scale, shards, 0, [])

        made, outputs = gather_and_scatter(out_grad, forward(2), beside, along, shards, 2)
        return outputs, *made

    cut = row_blocks - rows_per_step(row_blocks)
    head, tail = swap(weights[:cut]), swap(weights[cut:])

    def gathered(p, given, parts):
        return start_section(me, shards, given) if p == shards - 1 else None

    section, outputs = gather_and_scatter(out_grad, forward(1), gathered, along, shards, 1)
    ((mate_m,), *_) = along
    head, outputs = lax.optimization_barrier((head, outputs))
    made = update(*fixed, head, mate_m, section, [], scale, shards, 0, [])
    made = update(*fixed, tail, mate_m, section, [], scale, shards, cut, made)
    return outputs, *made


def body(hidden, out_grad, weights, momentum, block_cols, step_number):
    levels = lax.axis_size("replica").bit_length() - 1
    outputs, new_w, new_m = lax.switch(
        lax.rem(step_number[0], levels),
        [functools.partial(step_for, bit) for bit in range(levels)],
        hidden,
        out_grad,
        weights[0],
        momentum[0],
        block_cols,
    )
    return outputs, new_w[None], new_m[None]


def solution(mesh):
    return jax.shard_map(
        body,
        mesh=mesh,
        in_specs=(
            P("replica", "tensor"),
            P(("replica", "tensor"), None),
            P("replica", "tensor", None, None),
            P("replica", "tensor", None, None),
            P("tensor", None),
            P(),
        ),
        out_specs=(
            P(("replica", "tensor"), None),
            P("replica", "tensor", None, None),
            P("replica", "tensor", None, None),
        ),
        check_vma=False,
    )
```

time: 176 us -> 167 us (0.949)
  waiting for transfers between devices: 119 us -> 111 us
  starting transfers between devices: 32.8 us -> 25.5 us
  other arithmetic: 0.53 us -> 3.08 us
  local copies, waits for them, and re-layouts: 1.58 us -> 3.92 us
    ppermute x14 -> x11, waiting for transfers between devices: 119 us -> 111 us  [the longest x3 84.7 us: swap(): lax.ppermute(value, 'replica', [(i, i ^ 1 << bit) for i in range(replicas)])]
    ppermute x14 -> x11, starting transfers between devices: 32.8 us -> 25.5 us  [the longest x8 21 us: exchange(): return lax.ppermute(value, 'tensor', pairs + [(j, i) for i, j in pairs])]
    slice x0 -> x2, local copies, waits for them, and re-layouts: none -> 3.89 us  [step_for(): head, tail = (swap(weights[:cut]), swap(weights[cut:]))]
    add x3 -> x6, other arithmetic: 0.34 us -> 3.08 us  [gather_and_scatter(): got[h][1 - side] + part[side]]
    pallas_call x2 -> x5, Pallas kernels: 19.8 us -> 21.3 us  [the longest x2 11.2 us: update(): pl.pallas_call(functools.partial(update_kernel, scale, shards, first, cou...]
  transfers between devices with their start and end apart: 14 -> 11, of which waited for: 7 -> 7; matrix products, arithmetic and copies ran while one was open for 1% -> 4% of each run, Pallas kernels for 4% -> 11%
where the time goes in v2:
time: 167 us
  waiting for transfers between devices  111 us (66%)
  starting transfers between devices  25.5 us (15%)
  Pallas kernels  21.3 us (13%)
  local copies, waits for them, and re-layouts  3.92 us (2%)
  other arithmetic  3.08 us (2%)
    ppermute x3, waiting for transfers between devices, swap(): lax.ppermute(value, 'replica', [(i, i ^ 1 << bit) for i in range(replicas)])  84.7 us
    ppermute x8, waiting for transfers between devices, exchange(): return lax.ppermute(value, 'tensor', pairs + [(j, i) for i, j in pairs])  25.8 us
    ppermute x8, starting transfers between devices, exchange(): return lax.ppermute(value, 'tensor', pairs + [(j, i) for i, j in pairs])  21 us
    pallas_call x2, Pallas kernels, update(): pl.pallas_call(functools.partial(update_kernel, scale, shards, first, cou...  11.2 us
    pallas_call x1, Pallas kernels, forward_parts(): pl.pallas_call(functools.partial(forward_kernel, scale, shards, pieces),...  7.92 us
    ppermute x3, starting transfers between devices, swap(): lax.ppermute(value, 'replica', [(i, i ^ 1 << bit) for i in range(replicas)])  4.58 us
    slice x2, local copies, waits for them, and re-layouts, step_for(): head, tail = (swap(weights[:cut]), swap(weights[cut:]))  3.89 us
  transfers between devices with their start and end apart: 11, of which 7 were waited for; matrix products, arithmetic and copies ran while one was open for 4% of the time, Pallas kernels for 11%

profile of v2, /device:TPU:0, one launch (start us, length us, event | category | flops | bytes accessed | tf_op | source)
XLA Modules:
  0.0 166.6 jit_solution(13145519167599877552)
XLA Ops:
  1.3 165.1 %conditional.1 = (bf16[64,4096]{1,0:T(8,128)(2,1)}, bf16[14,128,1024]{2,1,0:T(8,128)(2,1)}, bf16[14,128,1024]{2,1,0:T(8,128)(2,1)}) conditional(s32[]{:T(128)} %bitcast.6, (bf16[64,4096]{1,0:T(8,128)(2,1)}, s32[14,8]{0,1:T(8,128)}, bf16[256,1792]{1,0:T(8,128)(2,1)}, bf16[14,128,1024]{2,1,0:T(8,128)(2,1)}, ...), branch_computations={%region_0.0_spmd, %region_1.0_spmd, %region_2.0_spmd} | conditional | flops 1577986 | bytes 95952208 | solution.py:298
  1.3 0.0 copy-start.10
  1.3 3.0 %collective-permute-start.3 = (bf16[14,128,1024]{2,1,0:T(8,128)(2,1)}, bf16[14,128,1024]{2,1,0:T(8,128)(2,1)}, u32[]{:S(2)}, u32[]{:S(2)}) collective-permute-start(bf16[14,128,1024]{2,1,0:T(8,128)(2,1)} %get-tuple-element.144.m_ref), channel_id=1, source_target_pairs={{0,8},{4,12},{8,0},{12,4},{16,24},{20,28},{24,16},{28,20},{1,9},{5... | collective-permute-start | bytes 11010056 | tf_op jit(solution)/shard_map/cond/branch_1_fun/ppermute | solution.py:257
  4.3 3.9 %slice.14 = bf16[12,128,1024]{2,1,0:T(8,128)(2,1)} slice(bf16[14,128,1024]{2,1,0:T(8,128)(2,1)} %get-tuple-element.133.w_ref), slice={[0:12], [0:128], [0:1024]} | slice | bytes 6291456 | tf_op jit(solution)/shard_map/cond/branch_1_fun/slice | solution.py:283
  8.2 0.0 collective-permute-start
  8.2 1.5 collective-permute-start.2
  9.7 4.2 %collective-permute-start.1 = (bf16[64,4096]{1,0:T(8,128)(2,1)}, bf16[64,4096]{1,0:T(8,128)(2,1)}, u32[]{:S(2)}, u32[]{:S(2)}) collective-permute-start(bf16[64,4096]{1,0:T(8,128)(2,1)} %get-tuple-element.134.refs_0_), channel_id=1, source_target_pairs={{0,1},{2,3},{1,0},{3,2},{4,5},{6,7},{5,4},{7,6},{8,9},{10,11},{9,8... | collective-permute-start | bytes 1572872 | tf_op jit(solution)/shard_map/cond/branch_1_fun/ppermute | solution.py:221
  13.8 7.9 %forward_parts.4 = (bf16[64,4096]{1,0:T(8,128)(2,1)S(1)}, bf16[64,4096]{1,0:T(8,128)(2,1)S(1)}, bf16[64,4096]{1,0:T(8,128)(2,1)S(1)}, bf16[64,4096]{1,0:T(8,128)...) custom-call(s32[1]{0:T(128)} %bitcast.2.me_ref, ...), custom_call_target="tpu_custom_call" | custom-call | flops 1024 | bytes 1024 | tf_op jit(solution)/shard_map/cond/branch_1_fun/forward_parts/pallas_call | solution.py:69
  21.8 3.5 %collective-permute-done.1.refs_1_ = bf16[64,4096]{1,0:T(8,128)(2,1)} collective-permute-done((bf16[64,4096]{1,0:T(8,128)(2,1)}, bf16[64,4096]{1,0:T(8,128)(2,1)}, u32[]{:S(2)}, u32[]{:S(2)}) %collective-permute-start.1) | collective-permute-done | bytes 524320 | tf_op jit(solution)/shard_map/cond/branch_1_fun/ppermute | solution.py:221
  25.2 59.6 %collective-permute-done.3.mate_m_ref = bf16[14,128,1024]{2,1,0:T(8,128)(2,1)} collective-permute-done((bf16[14,128,1024]{2,1,0:T(8,128)(2,1)}, bf16[14,128,1024]{2,1,0:T(8,128)(2,1)}, u32[]{:S(2)}, u32[]{:S(2)}) %collective-permute-start.3) | collective-permute-done | bytes 3670048 | tf_op jit(solution)/shard_map/cond/branch_1_fun/ppermute | solution.py:257
  84.8 1.2 add.61
  86.0 0.8 collective-permute-start.5
  86.8 1.4 add.60
  88.2 4.9 %collective-permute-start.4 = (bf16[64,4096]{1,0:T(8,128)(2,1)S(1)}, bf16[64,4096]{1,0:T(8,128)(2,1)S(1)}, u32[]{:S(2)}, u32[]{:S(2)}) collective-permute-start(bf16[64,4096]{1,0:T(8,128)(2,1)S(1)} %add.60), channel_id=1, source_target_pairs={{0,1},{2,3},{1,0},{3,2},{4,5},{6,7},{5,4},{7,6},{8,9},{10,11},{9,8... | collective-permute-start | bytes 1572872 | tf_op jit(solution)/shard_map/cond/branch_1_fun/ppermute | solution.py:221
  93.1 9.6 %collective-permute-done.4.refs_3_ = bf16[64,4096]{1,0:T(8,128)(2,1)S(1)} collective-permute-done((bf16[64,4096]{1,0:T(8,128)(2,1)S(1)}, bf16[64,4096]{1,0:T(8,128)(2,1)S(1)}, u32[]{:S(2)}, u32[]{:S(2)}) %collective-permute-start.4) | collective-permute-done | bytes 524320 | tf_op jit(solution)/shard_map/cond/branch_1_fun/ppermute | solution.py:221
  102.7 0.1 add.63
  102.9 0.9 collective-permute-start.7
  103.8 0.1 add.62
  103.9 3.5 %collective-permute-start.6 = (bf16[64,4096]{1,0:T(8,128)(2,1)S(1)}, bf16[64,4096]{1,0:T(8,128)(2,1)S(1)}, u32[]{:S(2)}, u32[]{:S(2)}) collective-permute-start(bf16[64,4096]{1,0:T(8,128)(2,1)S(1)} %add.62), channel_id=1, source_target_pairs={{0,1},{2,3},{1,0},{3,2},{4,5},{6,7},{5,4},{7,6},{8,9},{10,11},{9,8... | collective-permute-start | bytes 1572872 | tf_op jit(solution)/shard_map/cond/branch_1_fun/ppermute | solution.py:221
  107.4 8.4 %collective-permute-done.6.refs_5_ = bf16[64,4096]{1,0:T(8,128)(2,1)S(1)} collective-permute-done((bf16[64,4096]{1,0:T(8,128)(2,1)S(1)}, bf16[64,4096]{1,0:T(8,128)(2,1)S(1)}, u32[]{:S(2)}, u32[]{:S(2)}) %collective-permute-start.6) | collective-permute-done | bytes 524320 | tf_op jit(solution)/shard_map/cond/branch_1_fun/ppermute | solution.py:221
  115.8 0.1 add.65
  115.9 0.7 collective-permute-start.9
  116.6 0.1 add.64
  116.7 4.6 %collective-permute-start.8 = (bf16[64,4096]{1,0:T(8,128)(2,1)S(1)}, bf16[64,4096]{1,0:T(8,128)(2,1)S(1)}, u32[]{:S(2)}, u32[]{:S(2)}) collective-permute-start(bf16[64,4096]{1,0:T(8,128)(2,1)S(1)} %add.64), channel_id=1, source_target_pairs={{0,1},{2,3},{1,0},{3,2},{4,5},{6,7},{5,4},{7,6},{8,9},{10,11},{9,8... | collective-permute-start | bytes 1572872 | tf_op jit(solution)/shard_map/cond/branch_1_fun/ppermute | solution.py:221
  121.4 1.6 collective-permute-start.10
  123.0 1.3 start_section.4.section
  124.2 4.3 %collective-permute-done.8.refs_1_ = bf16[64,4096]{1,0:T(8,128)(2,1)S(1)} collective-permute-done((bf16[64,4096]{1,0:T(8,128)(2,1)S(1)}, bf16[64,4096]{1,0:T(8,128)(2,1)S(1)}, u32[]{:S(2)}, u32[]{:S(2)}) %collective-permute-start.8) | collective-permute-done | bytes 524320 | tf_op jit(solution)/shard_map/cond/branch_1_fun/ppermute | solution.py:221
  128.6 1.0 add_up.4
  129.6 22.6 %collective-permute-done.mate_w_ref = bf16[12,128,1024]{2,1,0:T(8,128)(2,1)S(1)} collective-permute-done((bf16[12,128,1024]{2,1,0:T(8,128)(2,1)}, bf16[12,128,1024]{2,1,0:T(8,128)(2,1)S(1)}, u32[]{:S(2)}, u32[]{:S(2)}) %collective-permute-start) | collective-permute-done | bytes 3145760 | tf_op jit(solution)/shard_map/cond/branch_1_fun/ppermute | solution.py:257
  152.1 7.8 %update.6 = (bf16[14,128,1024]{2,1,0:T(8,128)(2,1)}, bf16[14,128,1024]{2,1,0:T(8,128)(2,1)}) custom-call(s32[1]{0:T(128)} %bitcast.2.me_ref, s32[8,14]{1,0:T(8,128)S(1)} %bitcast.20, bf16[256,1792]{1,0:T(8,128)(2,1)S(1)} %copy-done.7, bf16[14,128,1024]{2,1,0:T(8,128)(2,1)S(1)} %copy-done.1, bf16[14,128,1024]{2,1,0:T(8,128)(2,1)S(1)} %copy-done.4, ...), custom_call_target="tpu_custom_call" | custom-call | flops 1024 | bytes 1024 | tf_op jit(solution)/shard_map/cond/branch_1_fun/update/pallas_call | solution.py:174
  159.9 2.6 %collective-permute-done.10.mate_w_ref = bf16[2,128,1024]{2,1,0:T(8,128)(2,1)S(1)} collective-permute-done((bf16[2,128,1024]{2,1,0:T(8,128)(2,1)S(1)}, bf16[2,128,1024]{2,1,0:T(8,128)(2,1)S(1)}, u32[]{:S(2)}, u32[]{:S(2)}) %collective-permute-start.10) | collective-permute-done | bytes 524320 | tf_op jit(solution)/shard_map/cond/branch_1_fun/ppermute | solution.py:257
  162.5 3.4 %update.7 = (bf16[14,128,1024]{2,1,0:T(8,128)(2,1)}, bf16[14,128,1024]{2,1,0:T(8,128)(2,1)}) custom-call(s32[1]{0:T(128)} %bitcast.2.me_ref, s32[8,14]{1,0:T(8,128)S(1)} %bitcast.21, bf16[256,1792]{1,0:T(8,128)(2,1)S(1)} %copy-done.7, bf16[14,128,1024]{2,1,0:T(8,128)(2,1)S(1)} %copy-done.1, ...), custom_call_target="tpu_custom_call", output_to_operand_aliasing={{0}: (8, {}), {1}: (9, {})} | custom-call | flops 1024 | bytes 1024 | tf_op jit(solution)/shard_map/cond/branch_1_fun/update/pallas_call | solution.py:174
  (12 shorter events, 0.1 us)
Async XLA Ops:
  1.3 12.5 %copy-start.10 = (s32[14,8]{0,1:T(8,128)S(1)}, s32[14,8]{0,1:T(8,128)}, u32[]{:S(2)}) copy-start(s32[14,8]{0,1:T(8,128)} %get-tuple-element.135) | copy-start | bytes 1348 | tf_op jit(solution)/shard_map/cond
  1.3 83.5 %collective-permute-start.3 = (bf16[14,128,1024]{2,1,0:T(8,128)(2,1)}, bf16[14,128,1024]{2,1,0:T(8,128)(2,1)}, u32[]{:S(2)}, u32[]{:S(2)}) collective-permute-start(bf16[14,128,1024]{2,1,0:T(8,128)(2,1)} %get-tuple-element.144.m_ref), channel_id=1, source_target_pairs={{0,8},{4,12},{8,0},{12,4},{16,24},{20,28},{24,16},{28,20},{1,9},{5... | collective-permute-start | bytes 11010056 | tf_op jit(solution)/shard_map/cond/branch_1_fun/ppermute | solution.py:257
  8.2 143.9 %collective-permute-start = (bf16[12,128,1024]{2,1,0:T(8,128)(2,1)}, bf16[12,128,1024]{2,1,0:T(8,128)(2,1)S(1)}, u32[]{:S(2)}, u32[]{:S(2)}) collective-permute-start(bf16[12,128,1024]{2,1,0:T(8,128)(2,1)} %slice.14), channel_id=1, source_target_pairs={{0,8},{4,12},{8,0},{12,4},{16,24},{20,28},{24,16},{28,20},{1,9},{5... | collective-permute-start | bytes 9437192 | tf_op jit(solution)/shard_map/cond/branch_1_fun/ppermute | solution.py:257
  8.2 13.6 %collective-permute-start.2 = (bf16[64,4096]{1,0:T(8,128)(2,1)}, bf16[64,4096]{1,0:T(8,128)(2,1)}, u32[]{:S(2)}, u32[]{:S(2)}) collective-permute-start(bf16[64,4096]{1,0:T(8,128)(2,1)} %get-tuple-element.134.refs_0_), channel_id=1, source_target_pairs={{1,2},{2,1},{5,6},{6,5},{9,10},{10,9},{13,14},{14,13},{17,18},{18,... | collective-permute-start | bytes 1572872 | tf_op jit(solution)/shard_map/cond/branch_1_fun/ppermute | solution.py:221
  9.7 15.6 %collective-permute-start.1 = (bf16[64,4096]{1,0:T(8,128)(2,1)}, bf16[64,4096]{1,0:T(8,128)(2,1)}, u32[]{:S(2)}, u32[]{:S(2)}) collective-permute-start(bf16[64,4096]{1,0:T(8,128)(2,1)} %get-tuple-element.134.refs_0_), channel_id=1, source_target_pairs={{0,1},{2,3},{1,0},{3,2},{4,5},{6,7},{5,4},{7,6},{8,9},{10,11},{9,8... | collective-permute-start | bytes 1572872 | tf_op jit(solution)/shard_map/cond/branch_1_fun/ppermute | solution.py:221
  86.0 35.4 %copy-start.1 = (bf16[14,128,1024]{2,1,0:T(8,128)(2,1)S(1)}, bf16[14,128,1024]{2,1,0:T(8,128)(2,1)}, u32[]{:S(2)}) copy-start(bf16[14,128,1024]{2,1,0:T(8,128)(2,1)} %get-tuple-element.133.w_ref) | copy-start | bytes 11010052 | tf_op jit(solution)/shard_map/cond
  86.0 7.1 %collective-permute-start.5 = (bf16[64,4096]{1,0:T(8,128)(2,1)S(1)}, bf16[64,4096]{1,0:T(8,128)(2,1)S(1)}, u32[]{:S(2)}, u32[]{:S(2)}) collective-permute-start(bf16[64,4096]{1,0:T(8,128)(2,1)S(1)} %add.61), channel_id=1, source_target_pairs={{1,2},{2,1},{5,6},{6,5},{9,10},{10,9},{13,14},{14,13},{17,18},{18,... | collective-permute-start | bytes 1572872 | tf_op jit(solution)/shard_map/cond/branch_1_fun/ppermute | solution.py:221
  88.2 14.5 %collective-permute-start.4 = (bf16[64,4096]{1,0:T(8,128)(2,1)S(1)}, bf16[64,4096]{1,0:T(8,128)(2,1)S(1)}, u32[]{:S(2)}, u32[]{:S(2)}) collective-permute-start(bf16[64,4096]{1,0:T(8,128)(2,1)S(1)} %add.60), channel_id=1, source_target_pairs={{0,1},{2,3},{1,0},{3,2},{4,5},{6,7},{5,4},{7,6},{8,9},{10,11},{9,8... | collective-permute-start | bytes 1572872 | tf_op jit(solution)/shard_map/cond/branch_1_fun/ppermute | solution.py:221
  102.9 4.5 %collective-permute-start.7 = (bf16[64,4096]{1,0:T(8,128)(2,1)S(1)}, bf16[64,4096]{1,0:T(8,128)(2,1)S(1)}, u32[]{:S(2)}, u32[]{:S(2)}) collective-permute-start(bf16[64,4096]{1,0:T(8,128)(2,1)S(1)} %add.63), channel_id=1, source_target_pairs={{1,2},{2,1},{5,6},{6,5},{9,10},{10,9},{13,14},{14,13},{17,18},{18,... | collective-permute-start | bytes 1572872 | tf_op jit(solution)/shard_map/cond/branch_1_fun/ppermute | solution.py:221
  103.9 11.9 %collective-permute-start.6 = (bf16[64,4096]{1,0:T(8,128)(2,1)S(1)}, bf16[64,4096]{1,0:T(8,128)(2,1)S(1)}, u32[]{:S(2)}, u32[]{:S(2)}) collective-permute-start(bf16[64,4096]{1,0:T(8,128)(2,1)S(1)} %add.62), channel_id=1, source_target_pairs={{0,1},{2,3},{1,0},{3,2},{4,5},{6,7},{5,4},{7,6},{8,9},{10,11},{9,8... | collective-permute-start | bytes 1572872 | tf_op jit(solution)/shard_map/cond/branch_1_fun/ppermute | solution.py:221
  115.9 8.3 %collective-permute-start.9 = (bf16[64,4096]{1,0:T(8,128)(2,1)S(1)}, bf16[64,4096]{1,0:T(8,128)(2,1)S(1)}, u32[]{:S(2)}, u32[]{:S(2)}) collective-permute-start(bf16[64,4096]{1,0:T(8,128)(2,1)S(1)} %add.65), channel_id=1, source_target_pairs={{1,2},{2,1},{5,6},{6,5},{9,10},{10,9},{13,14},{14,13},{17,18},{18,... | collective-permute-start | bytes 1572872 | tf_op jit(solution)/shard_map/cond/branch_1_fun/ppermute | solution.py:221
  116.7 11.8 %collective-permute-start.8 = (bf16[64,4096]{1,0:T(8,128)(2,1)S(1)}, bf16[64,4096]{1,0:T(8,128)(2,1)S(1)}, u32[]{:S(2)}, u32[]{:S(2)}) collective-permute-start(bf16[64,4096]{1,0:T(8,128)(2,1)S(1)} %add.64), channel_id=1, source_target_pairs={{0,1},{2,3},{1,0},{3,2},{4,5},{6,7},{5,4},{7,6},{8,9},{10,11},{9,8... | collective-permute-start | bytes 1572872 | tf_op jit(solution)/shard_map/cond/branch_1_fun/ppermute | solution.py:221
  121.4 30.7 %copy-start.4 = (bf16[14,128,1024]{2,1,0:T(8,128)(2,1)S(1)}, bf16[14,128,1024]{2,1,0:T(8,128)(2,1)}, u32[]{:S(2)}) copy-start(bf16[14,128,1024]{2,1,0:T(8,128)(2,1)} %get-tuple-element.144.m_ref) | copy-start | bytes 11010052 | tf_op jit(solution)/shard_map/cond
  121.4 30.7 %copy-start.7 = (bf16[256,1792]{1,0:T(8,128)(2,1)S(1)}, bf16[256,1792]{1,0:T(8,128)(2,1)}, u32[]{:S(2)}) copy-start(bf16[256,1792]{1,0:T(8,128)(2,1)} %get-tuple-element.136.hid_ref) | copy-start | bytes 2752516 | tf_op jit(solution)/shard_map/cond
  121.4 41.1 %collective-permute-start.10 = (bf16[2,128,1024]{2,1,0:T(8,128)(2,1)S(1)}, bf16[2,128,1024]{2,1,0:T(8,128)(2,1)S(1)}, u32[]{:S(2)}, u32[]{:S(2)}) collective-permute-start(bf16[2,128,1024]{2,1,0:T(8,128)(2,1)S(1)} %slice.15), channel_id=1, source_target_pairs={{0,8},{4,12},{8,0},{12,4},{16,24},{20,28},{24,16},{28,20},{1,9},{5... | collective-permute-start | bytes 1572872 | tf_op jit(solution)/shard_map/cond/branch_1_fun/ppermute | solution.py:257

commit v3 on v2

--- a/solution.py
+++ b/solution.py
@@ -10,7 +10,7 @@
 LAMBDA_DC = 1.0
 MOMENT_DECAY = 0.9
 LEARN_RATE = 0.2
-VMEM_LIMIT = 14 * 1024 * 1024
+MIB = 1024 * 1024
 LIGHT = pl.CostEstimate(flops=1024, bytes_accessed=1024, transcendentals=0)
 ANYWHERE = pl.BlockSpec(memory_space=pl.ANY)
 IN_VMEM = pl.BlockSpec(memory_space=pltpu.VMEM)
@@ -50,14 +50,21 @@
         for p in range(1, shards):
             kept += [(me + ahead * (shards - p), below <= p - 1), (me - ahead * (shards - p), above <= p - 1)]
         rows = parts[0].shape[0]
+        ends = []
         for number, part in enumerate(parts):
             owner, used = kept[number // pieces]
             factor = scale if used is None else jnp.where(used, scale, 0.0)
             place = jnp.clip(owner, 0, shards - 1) * pieces + number % pieces
             start = pl.multiple_of(place * rows, rows)
-            for col in range(total.shape[0]):
-                value = total[col, pl.ds(start, rows), :] * factor
-                part[:, col * block_size : (col + 1) * block_size] = value.astype(jnp.bfloat16)
+            ends.append((part, start, factor))
+
+        def finish(col, _):
+            to = pl.ds(pl.multiple_of(col * block_size, block_size), block_size)
+            for part, start, factor in ends:
+                part[:, to] = (total[col, pl.ds(start, rows), :] * factor).astype(jnp.bfloat16)
+            return 0
+
+        lax.fori_loop(0, total.shape[0], finish, 0)
 
 
 def forward_parts(me, cols, hidden, weights, scale, shards, pieces, model_width):
@@ -76,10 +83,10 @@
                 pl.BlockSpec((tokens, rows_step * block_size), lambda r, *_: (0, r)),
                 pl.BlockSpec((rows_step, block_size, width), lambda r, *_: (r, 0, 0)),
             ],
-            out_specs=[pl.BlockSpec((rows, model_width), lambda r, *_: (0, 0))] * count,
+            out_specs=[IN_VMEM] * count,
             scratch_shapes=[pltpu.VMEM((model_width // block_size, tokens, block_size), jnp.float32)],
         ),
-        compiler_params=pltpu.CompilerParams(vmem_limit_bytes=VMEM_LIMIT),
+        compiler_params=pltpu.CompilerParams(vmem_limit_bytes=10 * MIB),
         cost_estimate=LIGHT,
         name="forward_parts",
     )(me, cols, hidden, weights)
@@ -99,27 +106,33 @@
 
 
 def section_kernel(shards, labels, me_ref, *refs):
-    section, sem = refs[-2:]
-    put_shards(me_ref[0], shards, [(*a, r) for a, r in zip(labels, refs)], section, sem)
-
-
-def start_section(me, shards, given):
+    *given, whole, section, staged, sem = refs
+    copy = pltpu.make_async_copy(whole, staged, sem.at[len(given)])
+    copy.start()
+    put_shards(me_ref[0], shards, [(*a, r) for a, r in zip(labels, given)], section, sem)
+    copy.wait()
+
+
+def start_section(me, shards, given, whole):
     labels, arrays = [a for a, _ in given], [a for _, a in given]
     rows, width = arrays[0].shape
     return pl.pallas_call(
         functools.partial(section_kernel, shards, labels),
-        out_shape=jax.ShapeDtypeStruct((rows * labels[0][3] * shards, width), jnp.bfloat16),
+        out_shape=[
+            jax.ShapeDtypeStruct((rows * labels[0][3] * shards, width), jnp.bfloat16),
+            jax.ShapeDtypeStruct(whole.shape, whole.dtype),
+        ],
         grid_spec=pltpu.PrefetchScalarGridSpec(
             num_scalar_prefetch=1,
             grid=(),
-            in_specs=[ANYWHERE] * len(arrays),
-            out_specs=IN_VMEM,
-            scratch_shapes=[pltpu.SemaphoreType.DMA((len(arrays),))],
-        ),
-        compiler_params=pltpu.CompilerParams(vmem_limit_bytes=VMEM_LIMIT),
+            in_specs=[ANYWHERE] * (len(arrays) + 1),
+            out_specs=[IN_VMEM, IN_VMEM],
+            scratch_shapes=[pltpu.SemaphoreType.DMA((len(arrays) + 1,))],
+        ),
+        compiler_params=pltpu.CompilerParams(vmem_limit_bytes=4 * MIB),
         cost_estimate=LIGHT,
         name="start_section",
-    )(me, *arrays)
+    )(me, *arrays, whole)
 
 
 def update_kernel(scale, shards, first, count, labels, me_ref, cols_ref, hid_ref, w_ref, m_ref, mate_w_ref, mate_m_ref, section, *refs):
@@ -160,8 +173,9 @@
             copy.wait()
 
 
-def update(me, cols, hidden, weights, momentum, mate_w, mate_m, section, late, scale, shards, first, made):
-    count, block_size, width = mate_w.shape
+def update(me, cols, hidden, weights, momentum, mate_w, mate_m, section, late, scale, shards, first, count, made):
+    block_size, width = mate_w.shape[1:]
+    mate_first = first if mate_w.shape[0] == weights.shape[0] else 0
     shape = jax.ShapeDtypeStruct(weights.shape, jnp.bfloat16)
     labels, arrays = [a for a, _ in late], [a for _, a in late]
     aliases = {8 + len(arrays) + i: i for i in range(len(made))}
@@ -169,7 +183,7 @@
         aliases[7] = 2
     held = pltpu.VMEM((count, block_size, width), jnp.bfloat16)
     window = pl.BlockSpec((count, block_size, width), lambda i, *_: (first // count, 0, 0))
-    whole = pl.BlockSpec(mate_w.shape, lambda i, *_: (0, 0, 0))
+    mates = pl.BlockSpec((count, block_size, width), lambda i, *_: (mate_first // count, 0, 0))
     hid = pl.BlockSpec((hidden.shape[0], count * block_size), lambda i, *_: (0, first // count))
     new = pl.pallas_call(
         functools.partial(update_kernel, scale, shards, first, count, labels),
@@ -177,43 +191,47 @@
         grid_spec=pltpu.PrefetchScalarGridSpec(
             num_scalar_prefetch=2,
             grid=(1,),
-            in_specs=[hid, window, window, whole, window, IN_VMEM] + [ANYWHERE] * (len(arrays) + len(made)),
+            in_specs=[hid, window, window, mates, window, IN_VMEM] + [ANYWHERE] * (len(arrays) + len(made)),
             out_specs=[ANYWHERE, ANYWHERE] + [IN_VMEM] * bool(late),
             scratch_shapes=[held, held, pltpu.SemaphoreType.DMA((3, max(count, len(arrays))))],
         ),
         input_output_aliases=aliases,
-        compiler_params=pltpu.CompilerParams(vmem_limit_bytes=VMEM_LIMIT),
+        compiler_params=pltpu.CompilerParams(vmem_limit_bytes=16 * MIB),
         cost_estimate=LIGHT,
         name="update",
     )(me, cols, hidden, weights, momentum, mate_w, mate_m, section, *arrays, *made)
-    return new[:2]
+    return list(new)
 
 
 def add_kernel(*refs):
-    (*terms, total, held, sem) = refs
-    rows = terms[0].shape[0]
-    for h in range(len(terms) // 3):
-        for r in range(0, rows, 16):
-            values = [t[r : r + 16, :].astype(jnp.float32) for t in terms[3 * h : 3 * h + 3]]
-            held[h * rows + r : h * rows + r + 16, :] = sum(values).astype(jnp.bfloat16)
-    copy = pltpu.make_async_copy(held, total, sem)
-    copy.start()
-    copy.wait()
-
-
-def add_up(pieces):
-    rows, width = pieces[0][0].shape
-    shape = (rows * len(pieces), width)
+    (*done, own, got_a, got_b, total, held, sem) = refs
+    rows = own.shape[0]
+    copies = [
+        pltpu.make_async_copy(ref, total.at[pl.ds(h * rows, rows)], sem.at[h]) for h, ref in enumerate((*done, held))
+    ]
+    for copy in copies[:-1]:
+        copy.start()
+    for r in range(0, rows, 16):
+        at = slice(r, r + 16)
+        held[at, :] = sum(t[at, :].astype(jnp.float32) for t in (own, got_a, got_b)).astype(jnp.bfloat16)
+    copies[-1].start()
+    for copy in copies:
+        copy.wait()
+
+
+def add_up(done, terms):
+    rows, width = terms[0].shape
+    count = len(done) + 1
     return pl.pallas_call(
         add_kernel,
-        out_shape=jax.ShapeDtypeStruct(shape, jnp.bfloat16),
-        in_specs=[IN_VMEM] * (3 * len(pieces)),
+        out_shape=jax.ShapeDtypeStruct((rows * count, width), jnp.bfloat16),
+        in_specs=[ANYWHERE] * len(done) + [IN_VMEM] * 3,
         out_specs=pl.BlockSpec(memory_space=pltpu.HBM),
-        scratch_shapes=[pltpu.VMEM(shape, jnp.bfloat16), pltpu.SemaphoreType.DMA],
-        compiler_params=pltpu.CompilerParams(vmem_limit_bytes=VMEM_LIMIT),
+        scratch_shapes=[pltpu.VMEM((rows, width), jnp.bfloat16), pltpu.SemaphoreType.DMA((count,))],
+        compiler_params=pltpu.CompilerParams(vmem_limit_bytes=4 * MIB),
         cost_estimate=LIGHT,
         name="add_up",
-    )(*[a for piece in pieces for a in piece])
+    )(*done, *terms)
 
 
 def exchange(value, parity, shards):
@@ -223,24 +241,26 @@
 
 def gather_and_scatter(own, make_parts, after_phase, along, shards, pieces):
     rows = own.shape[0] // pieces
-    given, got = [((0, 0, 0, 1), own)], []
-    for h in range(pieces):
-        piece = own[h * rows : (h + 1) * rows]
-        got.append([exchange(piece, side, shards) for side in (0, 1)])
+    whole = [exchange(own, side, shards) for side in (0, 1)]
     parts = make_parts()
+    whole, parts, along[0] = lax.optimization_barrier((whole, parts, along[0]))
+    given = [((0, 0, 0, 1), own)] + [((1, side, 0, 1), whole[side]) for side in (0, 1)]
+    got = [[a[h * rows : (h + 1) * rows] for a in whole] for h in range(pieces)]
     for p in range(1, shards):
         for h in range(pieces):
-            got[h], parts, along[p - 1] = lax.optimization_barrier((got[h], parts, along[p - 1]))
-            given += [((p, side, h, pieces), got[h][side]) for side in (0, 1)]
+            if p > 1:
+                got[h], parts, along[p - 1] = lax.optimization_barrier((got[h], parts, along[p - 1]))
+                given += [((p, side, h, pieces), got[h][side]) for side in (0, 1)]
             part = [parts[(2 * p - 1 + side) * pieces + h] for side in (0, 1)]
             got[h] = [exchange(got[h][1 - side] + part[side], side, shards) for side in (0, 1)]
-        if p == shards - 1 and pieces > 1:
-            label, last = given[-1]
-            last, got[:-1] = lax.optimization_barrier((last, got[:-1]))
-            given[-1] = (label, last)
         result = after_phase(p, given, parts)
-    result, along[shards - 1], got = lax.optimization_barrier((result, along[shards - 1], got))
-    return result, add_up([(parts[h], *got[h]) for h in range(pieces)])
+    totals = []
+    for h in range(pieces):
+        result, along[shards - 1], got[h] = lax.optimization_barrier((result, along[shards - 1], got[h]))
+        if h < pieces - 1:
+            totals.append(sum(a.astype(jnp.float32) for a in (parts[h], *got[h])).astype(jnp.bfloat16))
+            result, totals = lax.optimization_barrier((result, totals))
+    return result, add_up(totals, (parts[pieces - 1], *got[-1]))
 
 
 def step_for(bit, hidden, out_grad, weights, momentum, block_cols):
@@ -267,14 +287,14 @@
         def beside(p, given, parts):
             if p == 1:
                 behind, _ = lax.optimization_barrier((weights, parts[0]))
-                along[1].append(swap(behind))
+                along[shards - 2].append(swap(behind))
             if p == shards - 2:
                 counted.append(len(given))
-                along[p].append(start_section(me, shards, given))
+                along[p] += start_section(me, shards, given, along[0][0])
             if p == shards - 1:
-                (mate_m,), (mate_w,) = along[:2]
-                (section,), (count,) = along[p - 1], counted
-                return update(*fixed, mate_w, mate_m, section, given[count:], scale, shards, 0, [])
+                (count,), (mate_w, section, mate_m) = counted, along[shards - 2]
+                late = given[count:]
+                return update(*fixed, mate_w, mate_m, section, late, scale, shards, 0, row_blocks, [])[:2]
 
         made, outputs = gather_and_scatter(out_grad, forward(2), beside, along, shards, 2)
         return outputs, *made
@@ -283,13 +303,12 @@
     head, tail = swap(weights[:cut]), swap(weights[cut:])
 
     def gathered(p, given, parts):
-        return start_section(me, shards, given) if p == shards - 1 else None
-
-    section, outputs = gather_and_scatter(out_grad, forward(1), gathered, along, shards, 1)
-    ((mate_m,), *_) = along
+        return start_section(me, shards, given, along[0][0]) if p == shards - 1 else None
+
+    (section, mate_m), outputs = gather_and_scatter(out_grad, forward(1), gathered, along, shards, 1)
     head, outputs = lax.optimization_barrier((head, outputs))
-    made = update(*fixed, head, mate_m, section, [], scale, shards, 0, [])
-    made = update(*fixed, tail, mate_m, section, [], scale, shards, cut, made)
+    made = update(*fixed, head, mate_m, section, [], scale, shards, 0, cut, [])
+    made = update(*fixed, tail, mate_m, section, [], scale, shards, cut, row_blocks - cut, made)
     return outputs, *made
 
 

time: 167 us -> 166 us (level)
    pallas_call x2, Pallas kernels: 11.2 us -> 8.33 us  [update(): pl.pallas_call(functools.partial(update_kernel, scale, shards, first, cou...]
    ppermute x3, waiting for transfers between devices: 84.7 us -> 86.8 us  [swap(): lax.ppermute(value, 'replica', [(i, i ^ 1 << bit) for i in range(replicas)])]
where the time goes in v3:
time: 166 us
  waiting for transfers between devices  111 us (67%)
  starting transfers between devices  25.4 us (15%)
  Pallas kernels  20.1 us (12%)
  local copies, waits for them, and re-layouts  3.92 us (2%)
  other arithmetic  3.08 us (2%)
    ppermute x3, waiting for transfers between devices, swap(): lax.ppermute(value, 'replica', [(i, i ^ 1 << bit) for i in range(replicas)])  86.8 us
    ppermute x8, waiting for transfers between devices, exchange(): return lax.ppermute(value, 'tensor', pairs + [(j, i) for i, j in pairs])  24.2 us
    ppermute x8, starting transfers between devices, exchange(): return lax.ppermute(value, 'tensor', pairs + [(j, i) for i, j in pairs])  20.7 us
    pallas_call x1, Pallas kernels, forward_parts(): pl.pallas_call(functools.partial(forward_kernel, scale, shards, pieces),...  8.39 us
    pallas_call x2, Pallas kernels, update(): pl.pallas_call(functools.partial(update_kernel, scale, shards, first, cou...  8.33 us
    ppermute x3, starting transfers between devices, swap(): lax.ppermute(value, 'replica', [(i, i ^ 1 << bit) for i in range(replicas)])  4.64 us
    slice x2, local copies, waits for them, and re-layouts, step_for(): head, tail = (swap(weights[:cut]), swap(weights[cut:]))  3.89 us
  transfers between devices with their start and end apart: 11, of which 7 were waited for; matrix products, arithmetic and copies ran while one was open for 4% of the time, Pallas kernels for 11%

profile of v3, /device:TPU:0, one launch (start us, length us, event | category | flops | bytes accessed | tf_op | source)
XLA Modules:
  0.0 165.6 jit_solution(12282591386749273903)
XLA Ops:
  1.3 164.1 %conditional.1 = (bf16[64,4096]{1,0:T(8,128)(2,1)}, bf16[14,128,1024]{2,1,0:T(8,128)(2,1)}, bf16[14,128,1024]{2,1,0:T(8,128)(2,1)}) conditional(s32[]{:T(128)} %bitcast.6, (s32[14,8]{0,1:T(8,128)}, bf16[64,4096]{1,0:T(8,128)(2,1)}, bf16[256,1792]{1,0:T(8,128)(2,1)}, bf16[14,128,1024]{2,1,0:T(8,128)(2,1)}, ...), branch_computations={%region_0.0_spmd, %region_1.0_spmd, %region_2.0_spmd} | conditional | flops 2363394 | bytes 95952208 | solution.py:317
  1.5 0.0 copy-start.11
  1.6 3.0 %collective-permute-start.14 = (bf16[14,128,1024]{2,1,0:T(8,128)(2,1)}, bf16[14,128,1024]{2,1,0:T(8,128)(2,1)}, u32[]{:S(2)}, u32[]{:S(2)}) collective-permute-start(bf16[14,128,1024]{2,1,0:T(8,128)(2,1)} %get-tuple-element.181.m_ref), channel_id=1, source_target_pairs={{0,16},{4,20},{8,24},{12,28},{16,0},{20,4},{24,8},{28,12},{1,17},{... | collective-permute-start | bytes 11010056 | tf_op jit(solution)/shard_map/cond/branch_2_fun/ppermute | solution.py:277
  4.6 3.9 %slice.22 = bf16[12,128,1024]{2,1,0:T(8,128)(2,1)} slice(bf16[14,128,1024]{2,1,0:T(8,128)(2,1)} %get-tuple-element.170.w_ref), slice={[0:12], [0:128], [0:1024]} | slice | bytes 6291456 | tf_op jit(solution)/shard_map/cond/branch_2_fun/slice | solution.py:303
  8.4 0.0 collective-permute-start.11
  8.5 1.5 collective-permute-start.13
  9.9 4.1 %collective-permute-start.12 = (bf16[64,4096]{1,0:T(8,128)(2,1)}, bf16[64,4096]{1,0:T(8,128)(2,1)}, u32[]{:S(2)}, u32[]{:S(2)}) collective-permute-start(bf16[64,4096]{1,0:T(8,128)(2,1)} %get-tuple-element.171.refs_0_), channel_id=1, source_target_pairs={{0,1},{2,3},{1,0},{3,2},{4,5},{6,7},{5,4},{7,6},{8,9},{10,11},{9,8... | collective-permute-start | bytes 1572872 | tf_op jit(solution)/shard_map/cond/branch_2_fun/ppermute | solution.py:239
  14.1 8.4 %forward_parts.5 = (bf16[64,4096]{1,0:T(8,128)(2,1)S(1)}, bf16[64,4096]{1,0:T(8,128)(2,1)S(1)}, bf16[64,4096]{1,0:T(8,128)(2,1)S(1)}, bf16[64,4096]{1,0:T(8,128)...) custom-call(s32[1]{0:T(128)} %bitcast.4.me_ref, ...), custom_call_target="tpu_custom_call" | custom-call | flops 1024 | bytes 1024 | tf_op jit(solution)/shard_map/cond/branch_2_fun/forward_parts/pallas_call | solution.py:76
  22.5 3.0 %collective-permute-done.12.refs_1_ = bf16[64,4096]{1,0:T(8,128)(2,1)} collective-permute-done((bf16[64,4096]{1,0:T(8,128)(2,1)}, bf16[64,4096]{1,0:T(8,128)(2,1)}, u32[]{:S(2)}, u32[]{:S(2)}) %collective-permute-start.12) | collective-permute-done | bytes 524320 | tf_op jit(solution)/shard_map/cond/branch_2_fun/ppermute | solution.py:239
  25.5 59.6 %collective-permute-done.14.refs_7_ = bf16[14,128,1024]{2,1,0:T(8,128)(2,1)} collective-permute-done((bf16[14,128,1024]{2,1,0:T(8,128)(2,1)}, bf16[14,128,1024]{2,1,0:T(8,128)(2,1)}, u32[]{:S(2)}, u32[]{:S(2)}) %collective-permute-start.14) | collective-permute-done | bytes 3670048 | tf_op jit(solution)/shard_map/cond/branch_2_fun/ppermute | solution.py:277
  85.1 1.2 add.73
  86.2 0.8 collective-permute-start.16
  87.1 1.4 add.72
  88.5 4.8 %collective-permute-start.15 = (bf16[64,4096]{1,0:T(8,128)(2,1)S(1)}, bf16[64,4096]{1,0:T(8,128)(2,1)S(1)}, u32[]{:S(2)}, u32[]{:S(2)}) collective-permute-start(bf16[64,4096]{1,0:T(8,128)(2,1)S(1)} %add.72), channel_id=1, source_target_pairs={{0,1},{2,3},{1,0},{3,2},{4,5},{6,7},{5,4},{7,6},{8,9},{10,11},{9,8... | collective-permute-start | bytes 1572872 | tf_op jit(solution)/shard_map/cond/branch_2_fun/ppermute | solution.py:239
  93.3 9.6 %collective-permute-done.15.refs_3_ = bf16[64,4096]{1,0:T(8,128)(2,1)S(1)} collective-permute-done((bf16[64,4096]{1,0:T(8,128)(2,1)S(1)}, bf16[64,4096]{1,0:T(8,128)(2,1)S(1)}, u32[]{:S(2)}, u32[]{:S(2)}) %collective-permute-start.15) | collective-permute-done | bytes 524320 | tf_op jit(solution)/shard_map/cond/branch_2_fun/ppermute | solution.py:239
  103.0 0.1 add.75
  103.1 0.7 collective-permute-start.18
  103.8 0.1 add.74
  103.9 3.5 %collective-permute-start.17 = (bf16[64,4096]{1,0:T(8,128)(2,1)S(1)}, bf16[64,4096]{1,0:T(8,128)(2,1)S(1)}, u32[]{:S(2)}, u32[]{:S(2)}) collective-permute-start(bf16[64,4096]{1,0:T(8,128)(2,1)S(1)} %add.74), channel_id=1, source_target_pairs={{0,1},{2,3},{1,0},{3,2},{4,5},{6,7},{5,4},{7,6},{8,9},{10,11},{9,8... | collective-permute-start | bytes 1572872 | tf_op jit(solution)/shard_map/cond/branch_2_fun/ppermute | solution.py:239
  107.4 8.4 %collective-permute-done.17.refs_5_ = bf16[64,4096]{1,0:T(8,128)(2,1)S(1)} collective-permute-done((bf16[64,4096]{1,0:T(8,128)(2,1)S(1)}, bf16[64,4096]{1,0:T(8,128)(2,1)S(1)}, u32[]{:S(2)}, u32[]{:S(2)}) %collective-permute-start.17) | collective-permute-done | bytes 524320 | tf_op jit(solution)/shard_map/cond/branch_2_fun/ppermute | solution.py:239
  115.8 0.1 add.77
  116.0 0.7 collective-permute-start.20
  116.7 0.1 add.76
  116.8 4.6 %collective-permute-start.19 = (bf16[64,4096]{1,0:T(8,128)(2,1)S(1)}, bf16[64,4096]{1,0:T(8,128)(2,1)S(1)}, u32[]{:S(2)}, u32[]{:S(2)}) collective-permute-start(bf16[64,4096]{1,0:T(8,128)(2,1)S(1)} %add.76), channel_id=1, source_target_pairs={{0,1},{2,3},{1,0},{3,2},{4,5},{6,7},{5,4},{7,6},{8,9},{10,11},{9,8... | collective-permute-start | bytes 1572872 | tf_op jit(solution)/shard_map/cond/branch_2_fun/ppermute | solution.py:239
  121.4 1.6 collective-permute-start.21
  123.0 2.4 %start_section.5 = (bf16[256,4096]{1,0:T(8,128)(2,1)S(1)}, bf16[14,128,1024]{2,1,0:T(8,128)(2,1)S(1)}) custom-call(s32[1]{0:T(128)} %bitcast.4.me_ref, bf16[64,4096]{1,0:T(8,128)(2,1)} %get-tuple-element.171.refs_0_, bf16[64,4096]{1,0:T(8,128)(2,1)} %collective-permute-done.12.refs_1_, bf16[64,4096]{1,0:T(8,128)(2,1)} %collective-permute-done.13.refs_2_, ...), custom_call_target="tpu_custom_call" | custom-call | flops 1024 | bytes 1024 | tf_op jit(solution)/shard_map/cond/branch_2_fun/start_section/pallas_call | solution.py:119
  125.4 3.2 %collective-permute-done.19.refs_1_ = bf16[64,4096]{1,0:T(8,128)(2,1)S(1)} collective-permute-done((bf16[64,4096]{1,0:T(8,128)(2,1)S(1)}, bf16[64,4096]{1,0:T(8,128)(2,1)S(1)}, u32[]{:S(2)}, u32[]{:S(2)}) %collective-permute-start.19) | collective-permute-done | bytes 524320 | tf_op jit(solution)/shard_map/cond/branch_2_fun/ppermute | solution.py:239
  128.6 1.0 add_up.5
  129.6 22.8 %collective-permute-done.11.mate_w_ref = bf16[12,128,1024]{2,1,0:T(8,128)(2,1)S(1)} collective-permute-done((bf16[12,128,1024]{2,1,0:T(8,128)(2,1)}, bf16[12,128,1024]{2,1,0:T(8,128)(2,1)S(1)}, u32[]{:S(2)}, u32[]{:S(2)}) %collective-permute-start.11) | collective-permute-done | bytes 3145760 | tf_op jit(solution)/shard_map/cond/branch_2_fun/ppermute | solution.py:277
  152.4 6.0 %update.8 = (bf16[14,128,1024]{2,1,0:T(8,128)(2,1)}, bf16[14,128,1024]{2,1,0:T(8,128)(2,1)}) custom-call(s32[1]{0:T(128)} %bitcast.4.me_ref, s32[8,14]{1,0:T(8,128)S(1)} %bitcast.23, bf16[256,1792]{1,0:T(8,128)(2,1)S(1)} %copy-done.8, bf16[14,128,1024]{2,1,0:T(8,128)(2,1)S(1)} %copy-done.2, bf16[14,128,1024]{2,1,0:T(8,128)(2,1)S(1)} %copy-done.5, ...), custom_call_target="tpu_custom_call" | custom-call | flops 1024 | bytes 1024 | tf_op jit(solution)/shard_map/cond/branch_2_fun/update/pallas_call | solution.py:188
  158.4 4.4 %collective-permute-done.21.mate_w_ref = bf16[2,128,1024]{2,1,0:T(8,128)(2,1)S(1)} collective-permute-done((bf16[2,128,1024]{2,1,0:T(8,128)(2,1)S(1)}, bf16[2,128,1024]{2,1,0:T(8,128)(2,1)S(1)}, u32[]{:S(2)}, u32[]{:S(2)}) %collective-permute-start.21) | collective-permute-done | bytes 524320 | tf_op jit(solution)/shard_map/cond/branch_2_fun/ppermute | solution.py:277
  162.8 2.3 %update.9 = (bf16[14,128,1024]{2,1,0:T(8,128)(2,1)}, bf16[14,128,1024]{2,1,0:T(8,128)(2,1)}) custom-call(s32[1]{0:T(128)} %bitcast.4.me_ref, s32[8,14]{1,0:T(8,128)S(1)} %bitcast.24, bf16[256,1792]{1,0:T(8,128)(2,1)S(1)} %copy-done.8, bf16[14,128,1024]{2,1,0:T(8,128)(2,1)S(1)} %copy-done.2, ...), custom_call_target="tpu_custom_call", output_to_operand_aliasing={{0}: (8, {}), {1}: (9, {})} | custom-call | flops 1024 | bytes 1024 | tf_op jit(solution)/shard_map/cond/branch_2_fun/update/pallas_call | solution.py:188
  (12 shorter events, 0.1 us)
Async XLA Ops:
  1.5 12.5 %copy-start.11 = (s32[14,8]{0,1:T(8,128)S(1)}, s32[14,8]{0,1:T(8,128)}, u32[]{:S(2)}) copy-start(s32[14,8]{0,1:T(8,128)} %get-tuple-element.172) | copy-start | bytes 1348 | tf_op jit(solution)/shard_map/cond
  1.6 83.5 %collective-permute-start.14 = (bf16[14,128,1024]{2,1,0:T(8,128)(2,1)}, bf16[14,128,1024]{2,1,0:T(8,128)(2,1)}, u32[]{:S(2)}, u32[]{:S(2)}) collective-permute-start(bf16[14,128,1024]{2,1,0:T(8,128)(2,1)} %get-tuple-element.181.m_ref), channel_id=1, source_target_pairs={{0,16},{4,20},{8,24},{12,28},{16,0},{20,4},{24,8},{28,12},{1,17},{... | collective-permute-start | bytes 11010056 | tf_op jit(solution)/shard_map/cond/branch_2_fun/ppermute | solution.py:277
  8.4 143.9 %collective-permute-start.11 = (bf16[12,128,1024]{2,1,0:T(8,128)(2,1)}, bf16[12,128,1024]{2,1,0:T(8,128)(2,1)S(1)}, u32[]{:S(2)}, u32[]{:S(2)}) collective-permute-start(bf16[12,128,1024]{2,1,0:T(8,128)(2,1)} %slice.22), channel_id=1, source_target_pairs={{0,16},{4,20},{8,24},{12,28},{16,0},{20,4},{24,8},{28,12},{1,17},{... | collective-permute-start | bytes 9437192 | tf_op jit(solution)/shard_map/cond/branch_2_fun/ppermute | solution.py:277
  8.5 14.0 %collective-permute-start.13 = (bf16[64,4096]{1,0:T(8,128)(2,1)}, bf16[64,4096]{1,0:T(8,128)(2,1)}, u32[]{:S(2)}, u32[]{:S(2)}) collective-permute-start(bf16[64,4096]{1,0:T(8,128)(2,1)} %get-tuple-element.171.refs_0_), channel_id=1, source_target_pairs={{1,2},{2,1},{5,6},{6,5},{9,10},{10,9},{13,14},{14,13},{17,18},{18,... | collective-permute-start | bytes 1572872 | tf_op jit(solution)/shard_map/cond/branch_2_fun/ppermute | solution.py:239
  9.9 15.5 %collective-permute-start.12 = (bf16[64,4096]{1,0:T(8,128)(2,1)}, bf16[64,4096]{1,0:T(8,128)(2,1)}, u32[]{:S(2)}, u32[]{:S(2)}) collective-permute-start(bf16[64,4096]{1,0:T(8,128)(2,1)} %get-tuple-element.171.refs_0_), channel_id=1, source_target_pairs={{0,1},{2,3},{1,0},{3,2},{4,5},{6,7},{5,4},{7,6},{8,9},{10,11},{9,8... | collective-permute-start | bytes 1572872 | tf_op jit(solution)/shard_map/cond/branch_2_fun/ppermute | solution.py:239
  86.2 35.2 %copy-start.2 = (bf16[14,128,1024]{2,1,0:T(8,128)(2,1)S(1)}, bf16[14,128,1024]{2,1,0:T(8,128)(2,1)}, u32[]{:S(2)}) copy-start(bf16[14,128,1024]{2,1,0:T(8,128)(2,1)} %get-tuple-element.170.w_ref) | copy-start | bytes 11010052 | tf_op jit(solution)/shard_map/cond
  86.2 7.1 %collective-permute-start.16 = (bf16[64,4096]{1,0:T(8,128)(2,1)S(1)}, bf16[64,4096]{1,0:T(8,128)(2,1)S(1)}, u32[]{:S(2)}, u32[]{:S(2)}) collective-permute-start(bf16[64,4096]{1,0:T(8,128)(2,1)S(1)} %add.73), channel_id=1, source_target_pairs={{1,2},{2,1},{5,6},{6,5},{9,10},{10,9},{13,14},{14,13},{17,18},{18,... | collective-permute-start | bytes 1572872 | tf_op jit(solution)/shard_map/cond/branch_2_fun/ppermute | solution.py:239
  88.5 14.5 %collective-permute-start.15 = (bf16[64,4096]{1,0:T(8,128)(2,1)S(1)}, bf16[64,4096]{1,0:T(8,128)(2,1)S(1)}, u32[]{:S(2)}, u32[]{:S(2)}) collective-permute-start(bf16[64,4096]{1,0:T(8,128)(2,1)S(1)} %add.72), channel_id=1, source_target_pairs={{0,1},{2,3},{1,0},{3,2},{4,5},{6,7},{5,4},{7,6},{8,9},{10,11},{9,8... | collective-permute-start | bytes 1572872 | tf_op jit(solution)/shard_map/cond/branch_2_fun/ppermute | solution.py:239
  103.1 4.3 %collective-permute-start.18 = (bf16[64,4096]{1,0:T(8,128)(2,1)S(1)}, bf16[64,4096]{1,0:T(8,128)(2,1)S(1)}, u32[]{:S(2)}, u32[]{:S(2)}) collective-permute-start(bf16[64,4096]{1,0:T(8,128)(2,1)S(1)} %add.75), channel_id=1, source_target_pairs={{1,2},{2,1},{5,6},{6,5},{9,10},{10,9},{13,14},{14,13},{17,18},{18,... | collective-permute-start | bytes 1572872 | tf_op jit(solution)/shard_map/cond/branch_2_fun/ppermute | solution.py:239
  103.9 11.9 %collective-permute-start.17 = (bf16[64,4096]{1,0:T(8,128)(2,1)S(1)}, bf16[64,4096]{1,0:T(8,128)(2,1)S(1)}, u32[]{:S(2)}, u32[]{:S(2)}) collective-permute-start(bf16[64,4096]{1,0:T(8,128)(2,1)S(1)} %add.74), channel_id=1, source_target_pairs={{0,1},{2,3},{1,0},{3,2},{4,5},{6,7},{5,4},{7,6},{8,9},{10,11},{9,8... | collective-permute-start | bytes 1572872 | tf_op jit(solution)/shard_map/cond/branch_2_fun/ppermute | solution.py:239
  116.0 9.5 %collective-permute-start.20 = (bf16[64,4096]{1,0:T(8,128)(2,1)S(1)}, bf16[64,4096]{1,0:T(8,128)(2,1)S(1)}, u32[]{:S(2)}, u32[]{:S(2)}) collective-permute-start(bf16[64,4096]{1,0:T(8,128)(2,1)S(1)} %add.77), channel_id=1, source_target_pairs={{1,2},{2,1},{5,6},{6,5},{9,10},{10,9},{13,14},{14,13},{17,18},{18,... | collective-permute-start | bytes 1572872 | tf_op jit(solution)/shard_map/cond/branch_2_fun/ppermute | solution.py:239
  116.8 11.8 %collective-permute-start.19 = (bf16[64,4096]{1,0:T(8,128)(2,1)S(1)}, bf16[64,4096]{1,0:T(8,128)(2,1)S(1)}, u32[]{:S(2)}, u32[]{:S(2)}) collective-permute-start(bf16[64,4096]{1,0:T(8,128)(2,1)S(1)} %add.76), channel_id=1, source_target_pairs={{0,1},{2,3},{1,0},{3,2},{4,5},{6,7},{5,4},{7,6},{8,9},{10,11},{9,8... | collective-permute-start | bytes 1572872 | tf_op jit(solution)/shard_map/cond/branch_2_fun/ppermute | solution.py:239
  121.4 31.0 %copy-start.5 = (bf16[14,128,1024]{2,1,0:T(8,128)(2,1)S(1)}, bf16[14,128,1024]{2,1,0:T(8,128)(2,1)}, u32[]{:S(2)}) copy-start(bf16[14,128,1024]{2,1,0:T(8,128)(2,1)} %get-tuple-element.181.m_ref) | copy-start | bytes 11010052 | tf_op jit(solution)/shard_map/cond
  121.4 30.9 %copy-start.8 = (bf16[256,1792]{1,0:T(8,128)(2,1)S(1)}, bf16[256,1792]{1,0:T(8,128)(2,1)}, u32[]{:S(2)}) copy-start(bf16[256,1792]{1,0:T(8,128)(2,1)} %get-tuple-element.173.hid_ref) | copy-start | bytes 2752516 | tf_op jit(solution)/shard_map/cond
  121.4 41.3 %collective-permute-start.21 = (bf16[2,128,1024]{2,1,0:T(8,128)(2,1)S(1)}, bf16[2,128,1024]{2,1,0:T(8,128)(2,1)S(1)}, u32[]{:S(2)}, u32[]{:S(2)}) collective-permute-start(bf16[2,128,1024]{2,1,0:T(8,128)(2,1)S(1)} %slice.23), channel_id=1, source_target_pairs={{0,16},{4,20},{8,24},{12,28},{16,0},{20,4},{24,8},{28,12},{1,17},{... | collective-permute-start | bytes 1572872 | tf_op jit(solution)/shard_map/cond/branch_2_fun/ppermute | solution.py:277
